TPU v7x, 128 devices: a whole 4x4x4 slice. The times are simulated.
128 devices in a mesh: seq: 16 (over y, z), head: 8 (over x, core).
Axes of the slice: x: 4, y: 4, z: 4, core: 2. Of those that a mesh axis runs over, the one named last changes fastest.
Arguments:
- inputs: bfloat16 [32768, 16384], P('seq', 'head'), may hold values from -6 to 6
- gates: bfloat16 [32768, 16384], P('seq', 'head'), may hold values from -6 to 6
- writes: bfloat16 [32768, 1024], P('seq', 'head'), may hold values from -2 to 2
- reads: bfloat16 [32768, 1024], P('seq', 'head'), may hold values from -2 to 2
- step_raw: float32 [128, 32768], P('head', 'seq'), may hold values from -3 to 3
- step_bias: float32 [128], P('head'), may hold values from -1 to 1
- decay_rate: float32 [128], P('head'), may hold values from 3e-05 to 0.06
- skip_gain: float32 [128], P('head'), may hold values from 0.5 to 2
- conv_inputs: bfloat16 [4, 16384], P(None, 'head'), may hold values from -3 to 3
- conv_writes: bfloat16 [4, 1024], P(None, 'head'), may hold values from -3 to 3
- conv_reads: bfloat16 [4, 1024], P(None, 'head'), may hold values from -3 to 3
- norm_gain: float32 [16384], P('head'), may hold values from 0.1 to 1.9
- positions: int32 [32768], P('seq'), may hold values from 0 to 32767, as said below
- segments: int32 [32768], replicated, may hold values from 0 to 5, never falling along the last dimension, each value on 1 to 10922 neighbouring positions
Outputs:
- outputs: bfloat16 [32768, 16384], P('seq', 'head')
Inputs may be any that keep to these rules, and one draw needn't show every extreme that they name: The rows of seq shard i are the positions of two blocks of 1024 positions each: block i and block 31 - i of the sequence, each in increasing order, the two blocks in either order. `segments`: never falling along the positions; each value is one document.
All inputs are finite; a program needn't handle non-finite values.
Results may differ from a plain program's by a relative error of at most 0.0065.
Values may be sent and summed in bfloat16 or wider, within the bound.
A program may use at most 256 MiB of HBM per device.

v0:
```python
import jax
import jax.numpy as jnp
from jax import lax
from jax.sharding import PartitionSpec as P

H = 128
P_SIZE = 128
N = 128
G = 8
BLOCK = 512


EPSILON = 1e-05


def padded(cells, sides, width):
    for axis, dim in sides:
        count = lax.axis_size(axis)
        ends = count - 1
        head = lax.slice_in_dim(cells, 0, width, axis=dim)
        tail = lax.slice_in_dim(cells, cells.shape[dim] - width, cells.shape[dim], axis=dim)
        cells = jnp.concatenate(
            [
                lax.ppermute(tail, axis, [(i, (i + 1) % count) for i in range(ends)]),
                cells,
                lax.ppermute(head, axis, [((i + 1) % count, i) for i in range(ends)]),
            ],
            axis=dim,
        )
    return cells


def carried_in(x, axis, combine, identity, reverse):
    size, position = (lax.axis_size(axis), lax.axis_index(axis))
    everything = jax.tree.map(lambda part: lax.all_gather(part, axis), x)
    start = jax.tree.map(
        lambda part, zero: jnp.broadcast_to(jnp.asarray(zero, part.dtype), part.shape), x, identity
    )

    def lap(k, before):
        at = size - 1 - k if reverse else k
        reached = at > position if reverse else at < position
        new = combine(before, jax.tree.map(lambda part: part[at], everything))
        return jax.tree.map(lambda a, b: jnp.where(reached, a, b), new, before)

    return lax.fori_loop(0, size, lap, start)


def convolve(window, taps, seg_window):
    length = window.shape[0] - 3
    summed = jnp.zeros((length, window.shape[1]), jnp.float32)
    for k in range(4):
        same_doc = (seg_window[k : k + length] == seg_window[3:])[:, None]
        term = window[k : k + length].astype(jnp.float32) * taps[k].astype(jnp.float32)
        summed = summed + jnp.where(same_doc, term, 0.0)
    return jax.nn.silu(summed).astype(jnp.bfloat16)


def block_parts(features, writes, reads, step_size, log_decay, seg_block, seg_before):
    length = features.shape[0]
    scores = jnp.einsum("tgn,sgn->gts", reads, writes, preferred_element_type=jnp.float32)
    cumulative = jnp.cumsum(log_decay, axis=2)
    spread = cumulative[:, :, :, None] - cumulative[:, :, None, :]
    indices = jnp.arange(length, dtype=jnp.int32)
    same_doc = (seg_block[:, None] == seg_block[None, :]) & (indices[None, :] <= indices[:, None])
    decay_mask = jnp.where(same_doc, jnp.exp(jnp.minimum(spread, 0.0)), 0.0)
    weights = (scores[:, None] * decay_mask * step_size[:, :, None, :]).astype(jnp.bfloat16)
    inner_part = jnp.einsum(
        "gets,sgep->tgep", weights, features, preferred_element_type=jnp.float32
    )
    keep_end = seg_block == seg_block[length - 1]
    tail_scale = jnp.where(
        keep_end, jnp.exp(cumulative[:, :, length - 1 :] - cumulative) * step_size, 0.0
    )
    write_scaled = (jnp.transpose(writes, (1, 0, 2))[:, None] * tail_scale[..., None]).astype(
        jnp.bfloat16
    )
    state_add = jnp.einsum(
        "sgep,gesn->gepn", features, write_scaled, preferred_element_type=jnp.float32
    )
    block_decay = jnp.where(
        seg_block[length - 1] == seg_before, jnp.exp(cumulative[:, :, length - 1]), 0.0
    )
    return (inner_part, state_add, block_decay, cumulative)


def block_inter(reads, cumulative, seg_block, seg_before, state_in):
    enter_mask = seg_block == seg_before
    read_scaled = (
        jnp.transpose(reads, (1, 0, 2))[:, None]
        * jnp.where(enter_mask, jnp.exp(cumulative), 0.0)[..., None]
    ).astype(jnp.bfloat16)
    return jnp.einsum(
        "gein,gepn->igep",
        read_scaled,
        state_in.astype(jnp.bfloat16),
        preferred_element_type=jnp.float32,
    )


def combine_seq(earlier, later):
    return (earlier[0] * later[0], later[0][..., None, None] * earlier[1] + later[1])


def on_device(
    inputs,
    gates,
    writes,
    reads,
    step_raw,
    step_bias,
    decay_rate,
    skip_gain,
    conv_inputs,
    conv_writes,
    conv_reads,
    norm_gain,
    positions,
    segments,
):
    tokens_here = inputs.shape[0]
    half_rows = tokens_here // 2
    heads_here = step_raw.shape[0]
    width_here = inputs.shape[1]
    per_group = H // G
    groups_here = heads_here // per_group
    state_width = groups_here * N
    first_start = positions[0]
    second_start = positions[half_rows]
    swapped = first_start > second_start
    seg_padded = jnp.concatenate([jnp.full((3,), -1, jnp.int32), segments])
    seg_first = lax.dynamic_slice_in_dim(seg_padded, first_start, half_rows + 3)
    seg_second = lax.dynamic_slice_in_dim(seg_padded, second_start, half_rows + 3)
    raw_rows = jnp.concatenate([inputs, writes, reads], axis=1)
    first_tail = raw_rows[half_rows - 3 : half_rows]
    second_tail = raw_rows[tokens_here - 3 :]
    low_tail = jnp.where(swapped, second_tail, first_tail)
    high_tail = jnp.where(swapped, first_tail, second_tail)
    rim_rows = jnp.concatenate([high_tail, low_tail], axis=0)
    extended = padded(rim_rows, (("seq", 0),), 3)
    is_last = lax.axis_index("seq") == lax.axis_size("seq") - 1
    prev_low = extended[:3]
    prev_high = jnp.where(is_last, low_tail, extended[9:12])
    prev_first = jnp.where(swapped, prev_high, prev_low)
    prev_second = jnp.where(swapped, prev_low, prev_high)
    conv_weight = jnp.concatenate([conv_inputs, conv_writes, conv_reads], axis=1)
    conv_first = convolve(
        jnp.concatenate([prev_first, raw_rows[:half_rows]], axis=0), conv_weight, seg_first
    )
    conv_second = convolve(
        jnp.concatenate([prev_second, raw_rows[half_rows:]], axis=0), conv_weight, seg_second
    )
    conv_all = jnp.concatenate([conv_first, conv_second], axis=0)
    feature_conv = conv_all[:, :width_here]
    write_conv = conv_all[:, width_here : width_here + state_width]
    read_conv = conv_all[:, width_here + state_width :]
    step_size = jax.nn.softplus(step_raw + step_bias[:, None])
    log_decay = -decay_rate[:, None] * step_size
    block_count = tokens_here // BLOCK
    per_half = block_count // 2
    seg_blocks = jnp.concatenate([seg_first[3:], seg_second[3:]]).reshape(block_count, BLOCK)
    seg_befores = jnp.concatenate(
        [seg_first[2 : 2 + half_rows : BLOCK], seg_second[2 : 2 + half_rows : BLOCK]]
    )
    feature_blocks = feature_conv.reshape(block_count, BLOCK, groups_here, per_group, P_SIZE)
    write_blocks = write_conv.reshape(block_count, BLOCK, groups_here, N)
    read_blocks = read_conv.reshape(block_count, BLOCK, groups_here, N)
    step_blocks = jnp.transpose(
        step_size.reshape(groups_here, per_group, block_count, BLOCK), (2, 0, 1, 3)
    )
    decay_blocks = jnp.transpose(
        log_decay.reshape(groups_here, per_group, block_count, BLOCK), (2, 0, 1, 3)
    )
    inner_part, state_add, block_decay, cumulative = lax.map(
        lambda a: block_parts(*a),
        (
            feature_blocks,
            write_blocks,
            read_blocks,
            step_blocks,
            decay_blocks,
            seg_blocks,
            seg_befores,
        ),
    )

    def fold_blocks(first_block):
        decay_total = jnp.ones_like(block_decay[0])
        state_total = jnp.zeros_like(state_add[0])
        for k in range(first_block, first_block + per_half):
            state_total = block_decay[k][..., None, None] * state_total + state_add[k]
            decay_total = decay_total * block_decay[k]
        return (decay_total, state_total)

    decay_first, state_first = fold_blocks(0)
    decay_second, state_second = fold_blocks(per_half)
    decay_low = jnp.where(swapped, decay_second, decay_first)
    decay_high = jnp.where(swapped, decay_first, decay_second)
    state_low = jnp.where(swapped, state_second, state_first)
    state_high = jnp.where(swapped, state_first, state_second)
    ones_decay = jnp.ones_like(decay_low)
    zero_state = jnp.zeros_like(state_low)
    prefix = carried_in((decay_low, state_low), "seq", combine_seq, (ones_decay, zero_state), False)

    def backward(earlier, later):
        low_part = combine_seq((later[0], later[1]), (earlier[0], earlier[1]))
        high_part = combine_seq((earlier[2], earlier[3]), (later[2], later[3]))
        return (low_part[0], low_part[1], high_part[0], high_part[1])

    suffix = carried_in(
        (decay_low, state_low, decay_high, state_high),
        "seq",
        backward,
        (ones_decay, zero_state, ones_decay, zero_state),
        True,
    )
    incoming_low = prefix[1]
    running = decay_low[..., None, None] * incoming_low + state_low
    running = suffix[0][..., None, None] * running + suffix[1]
    incoming_high = suffix[2][..., None, None] * running + suffix[3]
    incoming_first = jnp.where(swapped, incoming_high, incoming_low)
    incoming_second = jnp.where(swapped, incoming_low, incoming_high)
    entering = []
    running = incoming_first
    for k in range(per_half):
        entering.append(running)
        running = block_decay[k][..., None, None] * running + state_add[k]
    running = incoming_second
    for k in range(per_half, block_count):
        entering.append(running)
        running = block_decay[k][..., None, None] * running + state_add[k]
    entering = jnp.stack(entering, axis=0)
    inter_part = lax.map(
        lambda a: block_inter(*a), (read_blocks, cumulative, seg_blocks, seg_befores, entering)
    )
    mixed = (
        inner_part
        + inter_part
        + skip_gain.reshape(groups_here, per_group)[None, None, :, :, None]
        * feature_blocks.astype(jnp.float32)
    )
    mixed = mixed.reshape(tokens_here, width_here)
    gated_out = mixed * jax.nn.silu(gates.astype(jnp.float32))
    squares = jnp.sum(gated_out * gated_out, axis=1)
    square_sums = lax.psum(squares, "head")
    mean_square = square_sums / (H * P_SIZE)
    return (gated_out * lax.rsqrt(mean_square + EPSILON)[:, None] * norm_gain).astype(jnp.bfloat16)


def solution(mesh):
    return jax.shard_map(
        on_device,
        mesh=mesh,
        in_specs=(
            P("seq", "head"),
            P("seq", "head"),
            P("seq", "head"),
            P("seq", "head"),
            P("head", "seq"),
            P("head"),
            P("head"),
            P("head"),
            P(None, "head"),
            P(None, "head"),
            P(None, "head"),
            P("head"),
            P("seq"),
            P(),
        ),
        out_specs=P("seq", "head"),
        check_vma=False,
    )
```

profile of v0, /device:TPU:1, one launch (start us, length us, event | category | flops | bytes accessed | tf_op | source)
XLA Modules:
  0.0 668.8 jit_solution(11479884116843970879)
XLA Ops:
  7.9 8.4 %constant_dynamic-update-slice_fusion.5 = bf16[2048,2304]{1,0:T(8,128)(2,1)} fusion(bf16[2048,2048]{1,0:T(8,128)(2,1)} %param.22), kind=kLoop, calls=%fused_computation.145 | loop fusion | bytes 16777216
  20.3 4.4 collective-permute-start.1
  28.8 8.2 %fusion.74 = (bf16[1024,2304]{1,0:T(8,128)(2,1)}, bf16[1024,2304]{1,0:T(8,128)(2,1)}) fusion(bf16[2048,2304]{1,0:T(8,128)(2,1)} %constant_dynamic-update-slice_fusion.3), kind=kLoop, calls=%fused_computation.177 | loop fusion | bytes 18874368 | tf_op jit(solution)/shard_map/slice | solution.py:151
  41.6 15.7 %multiply_convert_fusion.13 = bf16[1024,2304]{1,0:T(8,128)(2,1)S(1)} fusion(bf16[1024,2304]{1,0:T(8,128)(2,1)} %get-tuple-element.675, bf16[3,2304]{1,0:T(4,128)(2,1)S(1)} %get-tuple-element.692, f32[2304]{0:T(1024)S(1)} %get-tuple-element.586, f32[2304]{0:T(1024)S(1)} %get-tuple-element.587, f32[2304]{0:T(1024)S(1)} %get-tuple-element.588, ...), kind=kLoop, calls=%fused_computation.85 | loop fusion | flops 66060288 | bytes 9490944 | tf_op jit(solution)/shard_map/convert_element_type | solution.py:56
  57.3 9.4 %multiply_convert_fusion.14 = bf16[1024,2304]{1,0:T(8,128)(2,1)S(1)} fusion(bf16[1024,2304]{1,0:T(8,128)(2,1)S(1)} %bitcast.254, bf16[3,2304]{1,0:T(4,128)(2,1)S(1)} %get-tuple-element.693, f32[2304]{0:T(1024)S(1)} %get-tuple-element.586, f32[2304]{0:T(1024)S(1)} %get-tuple-element.587, f32[2304]{0:T(1024)S(1)} %get-tuple-element.588, ...), kind=kLoop, calls=%fused_computation.86 | loop fusion | flops 66060288 | bytes 9490944 | tf_op jit(solution)/shard_map/convert_element_type | solution.py:56
  67.8 4.0 fusion.45
  71.8 9.8 %copy.59 = bf16[256,8,16,128]{3,2,1,0:T(8,128)(2,1)} copy(bf16[256,8,16,128]{3,1,2,0:T(8,128)(2,1)} %fusion.45) | data formatting | bytes 16777216
  81.6 7.1 %broadcast.285.clone2 = f32[4,512,1,16,128]{4,3,1,0,2:T(8,128)} broadcast(f32[]{:T(128)} %constant.134.clone.1), dimensions={} | broadcast | bytes 16777220 | tf_op jit(solution)/shard_map/broadcast.12
  88.8 150.0 %while.62 = (s32[]{:T(128)}, f32[4,512,1,16,128]{4,3,1,0,2:T(8,128)}, f32[4,1,16,128,128]{4,3,2,1,0:T(8,128)}, f32[4,1,16]{2,1,0:T(1,128)S(1)}, f32[4,1,16,512]{...) while((s32[]{:T(128)}, ...), condition=%wide.region_3.4_spmd, body=%wide.region_0.3_spmd.sunk | while | flops 1438483200 | bytes 47463296 | solution.py:174
  102.6 8.5 %fusion.97 = f32[1,512,1,16,128]{1,4,3,2,0:T(8,128)} fusion(f32[16,512]{1,0:T(8,128)} %bitcast.264, f32[16,512]{1,0:T(8,128)S(1)} %get-tuple-element.904, f32[512,512]{1,0:T(8,128)S(1)} %fusion.95, pred[512,512]{1,0:T(8,128)(4,1)S(1)} %fusion.96, bf16[1,512,1,16,128]{1,4,3,2,0:T(8,128)(2,1)} %copy.95), kind=kOutput, calls=%fused_computation.25.clone.1 | convolution fusion | flops 1098907648 | bytes 7667712 | tf_op jit(solution)/shard_map/while/body/eval_jaxpr/gets,sgep->tgep/dot_general | solution.py:68
  111.0 5.6 copy.96
  116.6 4.5 constant_dynamic-update-slice_fusion.12
  140.1 8.5 %fusion.97 = f32[1,512,1,16,128]{1,4,3,2,0:T(8,128)} fusion(f32[16,512]{1,0:T(8,128)} %bitcast.264, f32[16,512]{1,0:T(8,128)S(1)} %get-tuple-element.904, f32[512,512]{1,0:T(8,128)S(1)} %fusion.95, pred[512,512]{1,0:T(8,128)(4,1)S(1)} %fusion.96, bf16[1,512,1,16,128]{1,4,3,2,0:T(8,128)(2,1)} %copy.95), kind=kOutput, calls=%fused_computation.25.clone.1 | convolution fusion | flops 1098907648 | bytes 7667712 | tf_op jit(solution)/shard_map/while/body/eval_jaxpr/gets,sgep->tgep/dot_general | solution.py:68
  148.6 5.6 copy.96
  154.2 4.4 constant_dynamic-update-slice_fusion.12
  177.6 8.5 %fusion.97 = f32[1,512,1,16,128]{1,4,3,2,0:T(8,128)} fusion(f32[16,512]{1,0:T(8,128)} %bitcast.264, f32[16,512]{1,0:T(8,128)S(1)} %get-tuple-element.904, f32[512,512]{1,0:T(8,128)S(1)} %fusion.95, pred[512,512]{1,0:T(8,128)(4,1)S(1)} %fusion.96, bf16[1,512,1,16,128]{1,4,3,2,0:T(8,128)(2,1)} %copy.95), kind=kOutput, calls=%fused_computation.25.clone.1 | convolution fusion | flops 1098907648 | bytes 7667712 | tf_op jit(solution)/shard_map/while/body/eval_jaxpr/gets,sgep->tgep/dot_general | solution.py:68
  186.1 5.6 copy.96
  191.7 4.4 constant_dynamic-update-slice_fusion.12
  215.1 8.5 %fusion.97 = f32[1,512,1,16,128]{1,4,3,2,0:T(8,128)} fusion(f32[16,512]{1,0:T(8,128)} %bitcast.264, f32[16,512]{1,0:T(8,128)S(1)} %get-tuple-element.904, f32[512,512]{1,0:T(8,128)S(1)} %fusion.95, pred[512,512]{1,0:T(8,128)(4,1)S(1)} %fusion.96, bf16[1,512,1,16,128]{1,4,3,2,0:T(8,128)(2,1)} %copy.95), kind=kOutput, calls=%fused_computation.25.clone.1 | convolution fusion | flops 1098907648 | bytes 7667712 | tf_op jit(solution)/shard_map/while/body/eval_jaxpr/gets,sgep->tgep/dot_general | solution.py:68
  223.6 5.6 copy.96
  229.2 4.4 constant_dynamic-update-slice_fusion.12
  238.7 3.9 broadcast_select_fusion.5
  243.5 19.3 %all_gather.10 = f32[16,1,16]{2,1,0:T(1,128)S(1)} all-gather(f32[1,1,16]{2,1,0:T(1,128)S(1)} %get-tuple-element.699), channel_id=1, replica_groups=mesh['seq'=16,'head'=8] {'seq'}, dimensions={0}, use_global_device_ids=true | all-gather | bytes 1088 | tf_op jit(solution)/shard_map/all_gather | solution.py:35
  262.8 15.9 %all_gather.8 = f32[16,1,16]{2,1,0:T(1,128)S(1)} all-gather(f32[1,1,16]{2,1,0:T(1,128)S(1)} %get-tuple-element.700), channel_id=1, replica_groups=mesh['seq'=16,'head'=8] {'seq'}, dimensions={0}, use_global_device_ids=true | all-gather | bytes 1088 | tf_op jit(solution)/shard_map/all_gather | solution.py:35
  278.7 79.0 %all-gather.3.cloned.1.call-done = f32[16,1,16,128,128]{4,3,2,1,0:T(8,128)} async-done(((f32[1,1,16,128,128]{4,3,2,1,0:T(8,128)}), f32[16,1,16,128,128]{4,3,2,1,0:T(8,128)}) %all-gather.3.cloned.1.call-update) | async-done | bytes 16777232 | tf_op jit(solution)/shard_map/all_gather | solution.py:35
  357.7 113.2 %all-gather.5.cloned.1.call-done = f32[16,1,16,128,128]{4,3,2,1,0:T(8,128)} async-done(((f32[1,1,16,128,128]{4,3,2,1,0:T(8,128)}), f32[16,1,16,128,128]{4,3,2,1,0:T(8,128)}) %all-gather.5.cloned.1.call-update) | async-done | bytes 16777232 | tf_op jit(solution)/shard_map/all_gather | solution.py:35
  470.9 31.4 %while.64 = (s32[]{:T(128)}, f32[1,16]{1,0:T(1,128)S(1)}, f32[1,16,128,128]{3,2,1,0:T(8,128)S(1)}, f32[1,16]{1,0:T(1,128)S(1)}, f32[1,16,128,128]{3,2,1,0:T(8,12...) while((s32[]{:T(128)}, f32[1,16]{1,0:T(1,128)S(1)}, ...), condition=%wide.region_5.6_spmd.clone, body=%wide.region_4.5_spmd.clone.sunk | while | flops 2097256 | bytes 6292379 | solution.py:46
  502.3 23.9 %while.65 = (s32[]{:T(128)}, f32[1,16,128,128]{3,2,1,0:T(8,128)S(1)}, s32[]{:T(128)}, f32[16,1,16]{2,1,0:T(1,128)S(1)}, f32[16,1,16,128,128]{4,3,2,1,0:T(8,128)}, /*index=5*/s32[]{:T(128)}, s32[]{:T(128)}) while((s32[]{:T(128)}, f32[1,16,128,128]{3,2,1,0:T(8,128)S(1)}, s32[]{:T(128)}, f32[16,1,16]{2,1,0:T(1,128)S(1)}, ...), condition=%wide.region_7.8_spmd.clone, body=%wide.region_6.7_spmd.clone.sunk | while | flops 1048580 | bytes 3146025 | solution.py:46
  526.3 3.8 fusion.61
  530.9 7.2 %broadcast.285.clone = f32[4,512,1,16,128]{4,3,1,0,2:T(8,128)} broadcast(f32[]{:T(128)} %constant.134.clone.1), dimensions={} | broadcast | bytes 16777220 | tf_op jit(solution)/shard_map/broadcast.12
  538.1 67.0 %while.63 = (s32[]{:T(128)}, f32[4,512,1,16,128]{4,3,1,0,2:T(8,128)}, bf16[4,1,16,128,128]{4,3,2,1,0:T(8,128)(2,1)S(1)}, bf16[4,512,1,128]{3,1,2,0:T(8,128)(2,1)...) while((s32[]{:T(128)}, f32[4,512,1,16,128]{4,3,1,0,2:T(8,128)}, ...), condition=%wide.region_9.10_spmd, body=%wide.region_8.9_spmd.sunk | while | flops 270606848 | bytes 22318708 | solution.py:233
  541.9 3.1 convolution_bitcast_fusion.2
  545.0 5.5 copy.98
  550.4 4.4 constant_dynamic-update-slice_fusion.14
  558.7 3.1 convolution_bitcast_fusion.2
  561.7 5.5 copy.98
  567.2 4.4 constant_dynamic-update-slice_fusion.14
  575.4 3.1 convolution_bitcast_fusion.2
  578.5 5.5 copy.98
  584.0 4.4 constant_dynamic-update-slice_fusion.14
  592.2 3.1 convolution_bitcast_fusion.2
  595.3 5.5 copy.98
  600.7 4.4 constant_dynamic-update-slice_fusion.14
  605.1 13.9 %multiply_add_fusion = f32[4,512,1,16,128]{4,3,1,0,2:T(8,128)S(1)} fusion(bf16[4,512,1,16,128]{4,3,1,0,2:T(8,128)(2,1)} %get-tuple-element.1070, f32[4,512,1,16,128]{4,3,1,0,2:T(8,128)} %get-tuple-element.446, f32[4,512,1,16,128]{4,3,1,0,2:T(8,128)} %get-tuple-element.455, f32[16]{0:T(128)S(1)} %copy-done.12), kind=kLoop, calls=%fused_computation.80 | loop fusion | flops 16777216 | bytes 58720320 | tf_op jit(solution)/shard_map/add | solution.py:237
  619.0 5.7 copy-done
  624.7 8.4 %multiply_reduce_fusion = f32[2048]{0:T(1024)S(1)} fusion(bf16[2048,2048]{1,0:T(8,128)(2,1)} %param.23, f32[256,8,16,128]{3,2,1,0:T(8,128)S(1)} %bitcast.250), kind=kLoop, calls=%fused_computation.79 | loop fusion | flops 33552384 | bytes 25174016 | tf_op jit(solution)/shard_map/reduce_sum | solution.py:244
  633.1 12.7 %psum.7 = f32[2048]{0:T(1024)S(1)} all-reduce(f32[2048]{0:T(1024)S(1)} %multiply_reduce_fusion), channel_id=1, replica_groups=mesh['seq'=16,'head'=8] {'head'}, use_global_device_ids=true, to_apply=%region_11.12 | all-reduce | flops 2048 | bytes 16384 | tf_op jit(solution)/shard_map/psum | solution.py:245
  645.9 16.1 %multiply_convert_fusion.12 = bf16[2048,2048]{1,0:T(8,128)(2,1)} fusion(f32[2048]{0:T(1024)S(1)} %copy-done.8, f32[2048]{0:T(1024)S(1)} %add_rsqrt_fusion, bf16[2048,2048]{1,0:T(8,128)(2,1)} %param.23, f32[256,8,16,128]{3,2,1,0:T(8,128)} %bitcast.251), kind=kLoop, calls=%fused_computation.78 | loop fusion | flops 37748736 | bytes 33570816 | tf_op jit(solution)/shard_map/convert_element_type | solution.py:247
  (302 shorter events, 150.8 us)
Async XLA Ops:
  6.5 11.2 %copy-start.4 = (bf16[2048,128]{1,0:T(8,128)(2,1)S(1)}, bf16[2048,128]{1,0:T(8,128)(2,1)}, u32[]{:S(2)}) copy-start(bf16[2048,128]{1,0:T(8,128)(2,1)} %param.24) | copy-start | bytes 1572868
  6.5 12.1 %copy-start.5 = (bf16[2048,128]{1,0:T(8,128)(2,1)S(1)}, bf16[2048,128]{1,0:T(8,128)(2,1)}, u32[]{:S(2)}) copy-start(bf16[2048,128]{1,0:T(8,128)(2,1)} %param.25) | copy-start | bytes 1572868
  6.5 351.1 %all-gather.3.cloned.1.call-start = ((), (), s32[]{:S(2)}) async-start(), calls=%async_computation | async-start | bytes 17825792 | tf_op jit(solution)/shard_map/all_gather | solution.py:35
  20.3 21.3 %collective-permute-start.1 = (bf16[3,2304]{1,0:T(4,128)(2,1)S(1)}, bf16[3,2304]{1,0:T(4,128)(2,1)S(1)}, u32[]{:S(2)}, u32[]{:S(2)}) collective-permute-start(bf16[3,2304]{1,0:T(4,128)(2,1)S(1)} %get-tuple-element.678), channel_id=1, source_target_pairs={{0,8},{8,16},{16,24},{24,32},{32,40},{40,48},{48,56},{56,64},{64,7... | collective-permute-start | bytes 41480 | tf_op jit(solution)/shard_map/ppermute | solution.py:24
  24.7 16.9 %collective-permute-start = (bf16[3,2304]{1,0:T(4,128)(2,1)S(1)}, bf16[3,2304]{1,0:T(4,128)(2,1)S(1)}, u32[]{:S(2)}, u32[]{:S(2)}) collective-permute-start(bf16[3,2304]{1,0:T(4,128)(2,1)S(1)} %get-tuple-element.677), channel_id=1, source_target_pairs={{8,0},{16,8},{24,16},{32,24},{40,32},{48,40},{56,48},{64,56},{72,6... | collective-permute-start | bytes 41480 | tf_op jit(solution)/shard_map/ppermute | solution.py:26
  28.7 9.8 %copy-start.3 = (s32[32768]{0:T(1024)S(1)}, s32[32768]{0:T(1024)}, u32[]{:S(2)}) copy-start(s32[32768]{0:T(1024)} %param.35) | copy-start | bytes 393220
  28.7 9.9 %copy-start.7 = (bf16[4,2048]{1,0:T(4,128)(2,1)S(1)}, bf16[4,2048]{1,0:T(4,128)(2,1)}, u32[]{:S(2)}) copy-start(bf16[4,2048]{1,0:T(4,128)(2,1)} %param.30) | copy-start | bytes 49156
  28.7 9.9 %copy-start.9 = (bf16[4,128]{1,0:T(4,128)(2,1)S(1)}, bf16[4,128]{1,0:T(4,128)(2,1)}, u32[]{:S(2)}) copy-start(bf16[4,128]{1,0:T(4,128)(2,1)} %param.31) | copy-start | bytes 3076
  28.7 10.0 %copy-start.10 = (bf16[4,128]{1,0:T(4,128)(2,1)S(1)}, bf16[4,128]{1,0:T(4,128)(2,1)}, u32[]{:S(2)}) copy-start(bf16[4,128]{1,0:T(4,128)(2,1)} %param.32) | copy-start | bytes 3076
  28.7 10.4 %copy-start.13 = (f32[16]{0:T(128)S(1)}, f32[16]{0:T(128)}, u32[]{:S(2)}) copy-start(f32[16]{0:T(128)} %param.28) | copy-start | bytes 196
  28.8 10.5 %copy-start.6 = (f32[16,2048]{1,0:T(8,128)S(1)}, f32[16,2048]{1,0:T(8,128)}, u32[]{:S(2)}) copy-start(f32[16,2048]{1,0:T(8,128)} %param.26) | copy-start | bytes 393220
  28.8 10.5 %copy-start.11 = (f32[16]{0:T(128)S(1)}, f32[16]{0:T(128)}, u32[]{:S(2)}) copy-start(f32[16]{0:T(128)} %param.27) | copy-start | bytes 196
  37.0 20.3 %slice-start = ((s8[4718592]{0:T(1024)(128)(4,1)}), s8[524288]{0:T(1024)(128)(4,1)S(1)}, s32[]{:S(2)}) async-start(s8[4718592]{0:T(1024)(128)(4,1)} %bitcast.253), calls=%async_computation.2 | async-start | bytes 1048576
  41.6 15.7 %slice-start.1 = ((s8[4718592]{0:T(1024)(128)(4,1)}), s8[4194304]{0:T(1024)(128)(4,1)S(1)}, s32[]{:S(2)}) async-start(s8[4718592]{0:T(1024)(128)(4,1)} %bitcast.253), calls=%async_computation.3 | async-start | bytes 8388608
  111.0 11.1 %copy-start.1 = (bf16[1,512,1,16,128]{1,4,3,2,0:T(8,128)(2,1)S(1)}, bf16[1,512,1,16,128]{1,4,3,2,0:T(8,128)(2,1)}, u32[]{:S(2)}) copy-start(bf16[1,512,1,16,128]{1,4,3,2,0:T(8,128)(2,1)} %copy.95) | copy-start | bytes 6291460 | tf_op jit(solution)/shard_map/while
  148.6 11.0 %copy-start.1 = (bf16[1,512,1,16,128]{1,4,3,2,0:T(8,128)(2,1)S(1)}, bf16[1,512,1,16,128]{1,4,3,2,0:T(8,128)(2,1)}, u32[]{:S(2)}) copy-start(bf16[1,512,1,16,128]{1,4,3,2,0:T(8,128)(2,1)} %copy.95) | copy-start | bytes 6291460 | tf_op jit(solution)/shard_map/while
  186.1 10.9 %copy-start.1 = (bf16[1,512,1,16,128]{1,4,3,2,0:T(8,128)(2,1)S(1)}, bf16[1,512,1,16,128]{1,4,3,2,0:T(8,128)(2,1)}, u32[]{:S(2)}) copy-start(bf16[1,512,1,16,128]{1,4,3,2,0:T(8,128)(2,1)} %copy.95) | copy-start | bytes 6291460 | tf_op jit(solution)/shard_map/while
  223.6 10.9 %copy-start.1 = (bf16[1,512,1,16,128]{1,4,3,2,0:T(8,128)(2,1)S(1)}, bf16[1,512,1,16,128]{1,4,3,2,0:T(8,128)(2,1)}, u32[]{:S(2)}) copy-start(bf16[1,512,1,16,128]{1,4,3,2,0:T(8,128)(2,1)} %copy.95) | copy-start | bytes 6291460 | tf_op jit(solution)/shard_map/while
  242.7 228.2 %all-gather.5.cloned.1.call-start = ((), (), s32[]{:S(2)}) async-start(), calls=%async_computation.1 | async-start | bytes 17825792 | tf_op jit(solution)/shard_map/all_gather | solution.py:35
  526.3 3.8 copy-start.2
  538.1 67.0 %copy-start.12 = (f32[16]{0:T(128)S(1)}, f32[16]{0:T(128)}, u32[]{:S(2)}) copy-start(f32[16]{0:T(128)} %param.29) | copy-start | bytes 196
  619.0 5.7 copy-start
  624.7 21.1 %copy-start.8 = (f32[2048]{0:T(1024)S(1)}, f32[2048]{0:T(1024)}, u32[]{:S(2)}) copy-start(f32[2048]{0:T(1024)} %param.33) | copy-start | bytes 24580
Sparse Core Ops, SparseCore 0:
  242.8 114.8 all-gather.2
  359.8 111.0 all-gather.4
where the time goes:
time: 673 us; the launch traced here: 669 us
  waiting for transfers between devices  193 us (29%)
  local copies, waits for them, and re-layouts  182 us (27%)
  other arithmetic  153 us (23%)
  matrix products  61.2 us (9%)
  blocking collectives  47.9 us (7%)
  between operations  19.3 us (3%)
  loops' own time  6.75 us (1%)
    all_gather x2, waiting for transfers between devices, carried_in(): everything = jax.tree.map(lambda part: lax.all_gather(part, axis), x)  192 us
    dynamic_update_slice x24, local copies, waits for them, and re-layouts, on_device(): lax.map(lambda a: block_parts(*a), (feature_blocks, write_blocks, read_bl...  86.4 us
    select_n x48, other arithmetic, lap(): return jax.tree.map(lambda a, b: jnp.where(reached, a, b), new, before)  53.7 us
    dynamic_slice x32, local copies, waits for them, and re-layouts, on_device(): lax.map(lambda a: block_parts(*a), (feature_blocks, write_blocks, read_bl...  39.6 us
    all_gather x2, blocking collectives, carried_in(): everything = jax.tree.map(lambda part: lax.all_gather(part, axis), x)  35.2 us
    dot_general x4, matrix products, block_parts(): jnp.einsum('gets,sgep->tgep', weights, features, preferred_element_type=j...  33.9 us
    convert_element_type x2, other arithmetic, convolve(): return jax.nn.silu(summed).astype(jnp.bfloat16)  25.1 us
    unnamed x35, local copies, waits for them, and re-layouts  24.9 us
  transfers between devices with their start and end apart: 4, of which 2 were waited for; matrix products, arithmetic and copies ran while one was open for 2% of the time, Pallas kernels for 0%

commit v1 on v0

v1 whole, which is shorter than its diff:
```python
import functools

import jax
import jax.numpy as jnp
from jax import lax
from jax.experimental import pallas as pl
from jax.experimental.pallas import tpu as pltpu
from jax.sharding import PartitionSpec as P

H = 128
P_SIZE = 128
N = 128
G = 8
Q = 256
EPSILON = 1e-05
LOG2E = 1.4426950408889634
MESH = pl.DeviceIdType.MESH
MIB = 2**20
F32 = jnp.float32
BF16 = jnp.bfloat16

TAIL, CUM, ENTER, ENTER_HALF, INFO = 0, 16, 32, 48, 64


def silu_of_half(h):
    return h + h * jnp.tanh(h)


def conv_tile(ext, taps, cols, masked):
    total = ext[8:] * taps[3:4]
    for back in (1, 2, 3):
        term = pltpu.roll(ext, back, 0)[8:] * taps[3 - back : 4 - back]
        if masked:
            term = term * cols[:, INFO + back : INFO + back + 1]
        total = total + term
    return silu_of_half(total)


def local_kernel(
    flags,
    x_ref, w_ref, r_ref, step_ref, bias_ref, rate_ref, info_ref, halo_ref, taps_ref,
    feat_ref, wc_ref, rc_ref, cols_ref, brow_ref, sloc_ref, msg_ref,
    state, prev, carry, upper,
):
    i = pl.program_id(0)
    per_half = pl.num_programs(0) // 2
    at = lax.rem(i, per_half)
    width = x_ref.shape[1]
    heads = step_ref.shape[0]

    @pl.when(i == 0)
    def _():
        row = lax.broadcasted_iota(jnp.int32, (Q, Q), 0)
        col = lax.broadcasted_iota(jnp.int32, (Q, Q), 1)
        upper[...] = jnp.where(row <= col, 1.0, 0.0).astype(F32)

    @pl.when(at == 0)
    def _():
        state[...] = jnp.zeros_like(state)
        carry[...] = jnp.zeros_like(carry)
        prev[...] = halo_ref[0]

    step = jax.nn.softplus(step_ref[...] + bias_ref[...])
    decay = step * rate_ref[...]
    cum = jnp.dot(decay, upper[...], precision=lax.Precision.HIGHEST, preferred_element_type=F32)
    info = info_ref[...]
    seg, before, before_half, seg_end = info[0:1], info[4:5], info[5:6], info[6:7]
    cum_end = cum[:, Q - 1 : Q]
    tail = jnp.where(seg == seg_end, jnp.exp2(cum_end - cum) * step, 0.0)
    enter = jnp.where(seg == before, jnp.exp2(cum), 0.0)
    base = carry[:, 0:1]
    enter_half = jnp.where(seg == before_half, jnp.exp2(base + cum), 0.0)
    block_decay = enter[:, Q - 1 : Q]
    half_decay = enter_half[:, Q - 1 : Q]
    carry[...] = jnp.broadcast_to(base + cum_end, carry.shape)
    brow_ref[...] = cum - jnp.log2(step)
    fill = jnp.zeros((128 - INFO - 8, Q), F32)
    cols_ref[...] = jnp.transpose(
        jnp.concatenate([tail, cum, enter, enter_half, info, fill], axis=0)
    )

    def work(masked):
        cols = cols_ref[...]

        def conv(block, c0, c1):
            cur = block.astype(F32)
            ext = jnp.concatenate([prev[:, c0:c1], cur], axis=0)
            prev[:, c0:c1] = cur[Q - 8 :]
            return conv_tile(ext, taps_ref[:, c0:c1], cols, masked)

        wc = conv(w_ref[...], width, width + N)
        rc = conv(r_ref[...], width + N, width + 2 * N)
        wc_ref[...] = wc.astype(BF16)
        rc_ref[...] = rc.astype(BF16)
        wct = jnp.transpose(wc).astype(BF16)
        for pair in range(heads // 2):
            scaled = []
            for h in (2 * pair, 2 * pair + 1):
                c0, c1 = h * P_SIZE, (h + 1) * P_SIZE
                feat = conv(x_ref[:, c0:c1], c0, c1).astype(BF16)
                feat_ref[:, c0:c1] = feat
                scaled.append((feat.astype(F32) * cols[:, TAIL + h : TAIL + h + 1]).astype(BF16))
            add = jnp.dot(wct, jnp.concatenate(scaled, axis=1), preferred_element_type=F32)
            for k in (0, 1):
                h = 2 * pair + k
                c0, c1 = h * P_SIZE, (h + 1) * P_SIZE
                old = state[:, c0:c1]
                sloc_ref[0, :, c0:c1] = old.astype(BF16)
                new = old * block_decay[h : h + 1] + add[:, k * P_SIZE : (k + 1) * P_SIZE]
                state[:, c0:c1] = new

    @pl.when(flags[1 + i] == 0)
    def _():
        work(False)

    @pl.when(flags[1 + i] != 0)
    def _():
        work(True)

    @pl.when(at == per_half - 1)
    def _():
        for h in range(heads):
            msg_ref[h, 0, :N] = state[:, h * P_SIZE : (h + 1) * P_SIZE].astype(BF16)
            whole = jnp.broadcast_to(half_decay[h : h + 1], (8, P_SIZE))
            high = whole.astype(BF16).astype(F32)
            msg_ref[h, 0, N:] = jnp.concatenate([high, whole - high], axis=0).astype(BF16)


def exchange_kernel(n, msg_ref, out_ref, recv, back, s1, r1, s2, r2):
    me = lax.axis_index("seq")
    barrier = pltpu.get_barrier_semaphore()
    for k in range(1, n):
        pl.semaphore_signal(barrier, inc=1, device_id={"seq": lax.rem(me + k, n)}, device_id_type=MESH)
    pl.semaphore_wait(barrier, n - 1)

    def trip(src, dst, send, arrive):
        copies = []
        for k in range(1, n):
            to = lax.rem(me + k, n)
            copy = pltpu.make_async_remote_copy(
                src_ref=src.at[to], dst_ref=dst.at[me], send_sem=send.at[k], recv_sem=arrive.at[k],
                device_id={"seq": to}, device_id_type=MESH,
            )
            copy.start()
            copies.append(copy)
        return copies

    copies = trip(msg_ref, recv, s1, r1)
    recv[me] = msg_ref[me]
    for copy in copies:
        copy.wait()

    def advance(total, src, half):
        back[src, half] = total.astype(BF16)
        decay = recv[src, half, N : N + 1].astype(F32) + recv[src, half, N + 8 : N + 9].astype(F32)
        return total * decay + recv[src, half, :N].astype(F32)

    total = jnp.zeros((N, P_SIZE), F32)
    for src in range(n):
        total = advance(total, src, 0)
    for src in range(n - 1, -1, -1):
        total = advance(total, src, 1)
    copies = trip(back, out_ref, s2, r2)
    out_ref[me] = back[me]
    for copy in copies:
        copy.wait()


def inner_kernel(
    feat_ref, wc_ref, rc_ref, cols_ref, brow_ref, info_ref, sloc_ref, skip_ref, y_ref
):
    heads = brow_ref.shape[0]
    cols = cols_ref[...]
    rc = rc_ref[...]
    scores = lax.dot_general(rc, wc_ref[...], (((1,), (1,)), ((), ())), preferred_element_type=F32)
    row = lax.broadcasted_iota(jnp.int32, (Q, Q), 0)
    col = lax.broadcasted_iota(jnp.int32, (Q, Q), 1)
    keep = (cols[:, INFO : INFO + 1] == info_ref[0:1]) & (col <= row)
    scores = jnp.where(keep, scores, 0.0)
    half = Q // 2
    for pair in range(heads // 2):
        inter = jnp.dot(
            rc, sloc_ref[0, :, pair * 2 * P_SIZE : (pair + 1) * 2 * P_SIZE], preferred_element_type=F32
        )
        for k in (0, 1):
            h = 2 * pair + k
            c0, c1 = h * P_SIZE, (h + 1) * P_SIZE
            feat = feat_ref[:, c0:c1]
            cum = jnp.broadcast_to(cols[:, CUM + h : CUM + h + 1], (Q, P_SIZE))
            brow = brow_ref[h : h + 1, :]

            def tile(t, s):
                spread = cum[t * half : (t + 1) * half] - brow[:, s * half : (s + 1) * half]
                part = scores[t * half : (t + 1) * half, s * half : (s + 1) * half]
                return (part * jnp.exp2(spread)).astype(BF16)

            top = jnp.dot(tile(0, 0), feat[:half], preferred_element_type=F32)
            low = jnp.dot(
                jnp.concatenate([tile(1, 0), tile(1, 1)], axis=1), feat, preferred_element_type=F32
            )
            y = jnp.concatenate([top, low], axis=0)
            y = y + inter[:, k * P_SIZE : (k + 1) * P_SIZE] * cols[:, ENTER + h : ENTER + h + 1]
            y = y + feat.astype(F32) * skip_ref[:, c0:c1]
            y_ref[:, c0:c1] = y.astype(BF16)


def gate_kernel(swapped, y_ref, gate_ref, rc_ref, cols_ref, sin_ref, out_ref, sq_ref):
    heads = sin_ref.shape[0]
    cols = cols_ref[...]
    rc = rc_ref[...]
    squares = jnp.zeros((Q, P_SIZE), F32)
    for pair in range(heads // 2):
        both = jnp.concatenate([sin_ref[2 * pair, 0], sin_ref[2 * pair + 1, 0]], axis=1)
        inter = jnp.dot(rc, both, preferred_element_type=F32)
        for k in (0, 1):
            h = 2 * pair + k
            c0, c1 = h * P_SIZE, (h + 1) * P_SIZE
            y = y_ref[:, c0:c1].astype(F32)
            y = y + inter[:, k * P_SIZE : (k + 1) * P_SIZE] * cols[:, ENTER_HALF + h : ENTER_HALF + h + 1]
            gated = y * silu_of_half(gate_ref[:, c0:c1].astype(F32) * 0.5)
            squares = squares + gated * gated
            out_ref[:, c0:c1] = gated.astype(BF16)
    sums = jnp.sum(jnp.transpose(squares), axis=0, keepdims=True)
    sq_ref[0] = jnp.concatenate([sums[:, :128], sums[:, 128:]], axis=0)


def sum_kernel(n, mine_ref, out_ref, recv, send, arrive):
    me = lax.axis_index("head")
    barrier = pltpu.get_barrier_semaphore()
    for k in range(1, n):
        pl.semaphore_signal(barrier, inc=1, device_id={"head": lax.rem(me + k, n)}, device_id_type=MESH)
    pl.semaphore_wait(barrier, n - 1)
    copies = []
    for k in range(1, n):
        copy = pltpu.make_async_remote_copy(
            src_ref=mine_ref, dst_ref=recv.at[k], send_sem=send.at[k], recv_sem=arrive.at[k],
            device_id={"head": lax.rem(me + k, n)}, device_id_type=MESH,
        )
        copy.start()
        copies.append(copy)
    total = mine_ref[...]
    for k in range(1, n):
        copies[k - 1].wait()
        total = total + recv[k]
    out_ref[...] = lax.rsqrt(total / (H * P_SIZE) + EPSILON)


def norm_kernel(gated_ref, scale_ref, gain_ref, out_ref):
    scale = scale_ref[0]
    row = jnp.concatenate([scale[0:1], scale[1:2]], axis=1)
    col = jnp.transpose(jnp.broadcast_to(row, (128, Q)))
    for c in range(gated_ref.shape[1] // 128):
        c0, c1 = c * 128, (c + 1) * 128
        out_ref[:, c0:c1] = (gated_ref[:, c0:c1].astype(F32) * col * gain_ref[:, c0:c1]).astype(BF16)


def on_device(
    inputs, gates, writes, reads, step_raw, step_bias, decay_rate, skip_gain,
    conv_inputs, conv_writes, conv_reads, norm_gain, positions, segments,
):
    tokens, width = inputs.shape
    heads = step_raw.shape[0]
    half_rows = tokens // 2
    chunks = tokens // Q
    per_half = chunks // 2
    n_seq, n_head = lax.axis_size("seq"), lax.axis_size("head")
    first_start, second_start = positions[0], positions[half_rows]
    swapped = first_start > second_start

    def tail_rows(end):
        parts = [a[end - 8 : end] for a in (inputs, writes, reads)]
        return jnp.concatenate(parts, axis=1)

    first_tail, second_tail = tail_rows(half_rows), tail_rows(tokens)
    low_tail = jnp.where(swapped, second_tail, first_tail)
    high_tail = jnp.where(swapped, first_tail, second_tail)
    ends = n_seq - 1
    prev_low = lax.ppermute(low_tail, "seq", [(i, i + 1) for i in range(ends)])
    prev_high = lax.ppermute(high_tail, "seq", [(i + 1, i) for i in range(ends)])
    prev_high = jnp.where(lax.axis_index("seq") == ends, low_tail, prev_high)
    halo = jnp.stack(
        [jnp.where(swapped, prev_high, prev_low), jnp.where(swapped, prev_low, prev_high)]
    ).astype(F32)

    seg_padded = jnp.concatenate([jnp.full((3,), -1, jnp.int32), segments])
    windows = jnp.stack(
        [lax.dynamic_slice_in_dim(seg_padded, s, half_rows + 3) for s in (first_start, second_start)]
    )
    seg = windows[:, 3:]
    same = [seg == windows[:, 3 - k : 3 - k + half_rows] for k in (1, 2, 3)]
    before = jnp.broadcast_to(windows[:, 2 : 2 + half_rows : Q, None], (2, per_half, Q))
    seg_end = jnp.broadcast_to(seg[:, Q - 1 :: Q, None], (2, per_half, Q))
    before_half = jnp.broadcast_to(windows[:, 2:3], (2, half_rows))
    info = jnp.stack(
        [a.reshape(tokens).astype(F32) for a in (seg, *same, before, before_half, seg_end, jnp.zeros_like(seg))]
    )
    broken = jnp.any(~same[2].reshape(chunks, Q), axis=1)
    flags = jnp.concatenate([swapped[None], broken]).astype(jnp.int32)
    taps = jnp.concatenate([conv_inputs, conv_writes, conv_reads], axis=1).astype(F32) * 0.5
    taps = jnp.concatenate([taps, jnp.zeros_like(taps)], axis=0)

    rows = lambda cols: pl.BlockSpec((Q, cols), lambda i, *_: (i, 0))
    lanes = lambda n: pl.BlockSpec((n, Q), lambda i, *_: (0, i))
    whole = lambda *shape: pl.BlockSpec(shape, lambda i, *_: (0,) * len(shape))
    params = pltpu.CompilerParams(vmem_limit_bytes=48 * MIB)
    wide = width + 2 * N
    message = N + 16

    feat, wc, rc, cols, brow, sloc, msg = pl.pallas_call(
        local_kernel,
        grid_spec=pltpu.PrefetchScalarGridSpec(
            num_scalar_prefetch=1,
            grid=(chunks,),
            in_specs=[
                rows(width), rows(N), rows(N), lanes(heads), whole(heads, 1), whole(heads, 1), lanes(8),
                pl.BlockSpec((1, 8, wide), lambda i, f: (i // per_half, 0, 0)), whole(8, wide),
            ],
            out_specs=[
                rows(width), rows(N), rows(N), rows(128), lanes(heads),
                pl.BlockSpec((1, N, width), lambda i, f: (i, 0, 0)),
                pl.BlockSpec((heads, 1, message, P_SIZE), lambda i, f: (0, (i // per_half) ^ f[0], 0, 0)),
            ],
            scratch_shapes=[
                pltpu.VMEM((N, width), F32), pltpu.VMEM((8, wide), F32),
                pltpu.VMEM((heads, 128), F32), pltpu.VMEM((Q, Q), F32),
            ],
        ),
        out_shape=[
            jax.ShapeDtypeStruct((tokens, width), BF16),
            jax.ShapeDtypeStruct((tokens, N), BF16),
            jax.ShapeDtypeStruct((tokens, N), BF16),
            jax.ShapeDtypeStruct((tokens, 128), F32),
            jax.ShapeDtypeStruct((heads, tokens), F32),
            jax.ShapeDtypeStruct((chunks, N, width), BF16),
            jax.ShapeDtypeStruct((heads, 2, message, P_SIZE), BF16),
        ],
        compiler_params=params,
        name="local",
    )(
        flags, inputs, writes, reads, step_raw, step_bias[:, None], -LOG2E * decay_rate[:, None],
        info, halo, taps,
    )

    vmem = pl.BlockSpec(memory_space=pltpu.VMEM)
    entering = pl.pallas_call(
        functools.partial(exchange_kernel, n_seq),
        in_specs=[vmem],
        out_specs=vmem,
        out_shape=jax.ShapeDtypeStruct((n_seq, 2, N, P_SIZE), BF16),
        scratch_shapes=[
            pltpu.VMEM((n_seq, 2, message, P_SIZE), BF16), pltpu.VMEM((n_seq, 2, N, P_SIZE), BF16),
        ] + [pltpu.SemaphoreType.DMA((n_seq,))] * 4,
        compiler_params=pltpu.CompilerParams(
            collective_id=0, has_side_effects=True, vmem_limit_bytes=32 * MIB
        ),
        name="exchange",
    )(msg)

    y = pl.pallas_call(
        inner_kernel,
        grid=(chunks,),
        in_specs=[
            rows(width), rows(N), rows(N), rows(128), lanes(heads), lanes(8),
            pl.BlockSpec((1, N, width), lambda i: (i, 0, 0)), whole(1, width),
        ],
        out_specs=rows(width),
        out_shape=jax.ShapeDtypeStruct((tokens, width), BF16),
        compiler_params=params,
        name="inner",
    )(feat, wc, rc, cols, brow, info, sloc, jnp.repeat(skip_gain, P_SIZE)[None])

    gated, squares = pl.pallas_call(
        gate_kernel,
        grid_spec=pltpu.PrefetchScalarGridSpec(
            num_scalar_prefetch=1,
            grid=(chunks,),
            in_specs=[
                rows(width), rows(width), rows(N), rows(128),
                pl.BlockSpec((heads, 1, N, P_SIZE), lambda i, f: (0, (i // per_half) ^ f[0], 0, 0)),
            ],
            out_specs=[rows(width), pl.BlockSpec((1, Q // 128, 128), lambda i, f: (i, 0, 0))],
        ),
        out_shape=[
            jax.ShapeDtypeStruct((tokens, width), BF16),
            jax.ShapeDtypeStruct((chunks, Q // 128, 128), F32),
        ],
        compiler_params=params,
        name="gate",
    )(flags, y, gates, rc, cols, entering)

    scale = pl.pallas_call(
        functools.partial(sum_kernel, n_head),
        in_specs=[vmem],
        out_specs=vmem,
        out_shape=jax.ShapeDtypeStruct(squares.shape, F32),
        scratch_shapes=[pltpu.VMEM((n_head, *squares.shape), F32)] + [pltpu.SemaphoreType.DMA((n_head,))] * 2,
        compiler_params=pltpu.CompilerParams(collective_id=1, has_side_effects=True),
        name="sum",
    )(squares)

    return pl.pallas_call(
        norm_kernel,
        grid=(chunks,),
        in_specs=[rows(width), pl.BlockSpec((1, Q // 128, 128), lambda i: (i, 0, 0)), whole(1, width)],
        out_specs=rows(width),
        out_shape=jax.ShapeDtypeStruct((tokens, width), BF16),
        compiler_params=params,
        name="norm",
    )(gated, scale, norm_gain[None])


def solution(mesh):
    return jax.shard_map(
        on_device,
        mesh=mesh,
        in_specs=(
            P("seq", "head"), P("seq", "head"), P("seq", "head"), P("seq", "head"), P("head", "seq"),
            P("head"), P("head"), P("head"), P(None, "head"), P(None, "head"), P(None, "head"),
            P("head"), P("seq"), P(),
        ),
        out_specs=P("seq", "head"),
        check_vma=False,
    )
```

time: 673 us -> 133 us (0.20)
  waiting for transfers between devices: 193 us -> 0.01 us
  local copies, waits for them, and re-layouts: 182 us -> 9.38 us
  other arithmetic: 153 us -> 2.08 us
  Pallas kernels: 0 us -> 109 us
  matrix products: 61.2 us -> 0 us
  blocking collectives: 47.9 us -> 0 us
  between operations: 19.3 us -> 5.06 us
  loops' own time: 6.75 us -> 0 us
    all_gather x2 -> x0, waiting for transfers between devices: 192 us -> none  [carried_in(): everything = jax.tree.map(lambda part: lax.all_gather(part, axis), x)]
    pallas_call x0 -> x6, Pallas kernels: none -> 109 us  [the longest x1 37.9 us: on_device(): pl.pallas_call(functools.partial(exchange_kernel, n_seq), in_specs=[vmem]...]
    dynamic_update_slice x24 -> x0, local copies, waits for them, and re-layouts: 86.4 us -> none  [on_device(): lax.map(lambda a: block_parts(*a), (feature_blocks, write_blocks, read_bl...]
    dot_general x16 -> x0, matrix products: 61.2 us -> none  [the longest x4 33.9 us: block_parts(): jnp.einsum('gets,sgep->tgep', weights, features, preferred_element_type=j...]
    select_n x63 -> x0, other arithmetic: 59.6 us -> none  [the longest x48 53.7 us: lap(): return jax.tree.map(lambda a, b: jnp.where(reached, a, b), new, before)]
    convert_element_type x11 -> x5, other arithmetic: 48.6 us -> 0.29 us  [the longest x3 0.2 us: on_device(): a.reshape(tokens).astype(F32)]
    dynamic_slice x33 -> x1, local copies, waits for them, and re-layouts: 39.7 us -> 0.81 us  [on_device(): lax.dynamic_slice_in_dim(seg_padded, s, half_rows + 3)]
    all_gather x2 -> x0, blocking collectives: 35.2 us -> none  [carried_in(): everything = jax.tree.map(lambda part: lax.all_gather(part, axis), x)]
  transfers between devices with their start and end apart: 4 -> 2, of which waited for: 2 -> 0; matrix products, arithmetic and copies ran while one was open for 2% -> 3% of each run, Pallas kernels for 0% -> 0%
where the time goes in v1:
time: 133 us; the launch traced here: 132 us
  Pallas kernels  109 us (82%)
  local copies, waits for them, and re-layouts  9.38 us (7%)
  starting transfers between devices  6.29 us (5%)
  between operations  5.06 us (4%)
  other arithmetic  2.08 us (2%)
    pallas_call x1, Pallas kernels, on_device(): pl.pallas_call(functools.partial(exchange_kernel, n_seq), in_specs=[vmem]...  37.9 us
    pallas_call x1, Pallas kernels, on_device(): pl.pallas_call(local_kernel, grid_spec=pltpu.PrefetchScalarGridSpec(num_s...  23.9 us
    pallas_call x1, Pallas kernels, on_device(): pl.pallas_call(inner_kernel, grid=(chunks,), in_specs=[rows(width), rows(...  15.3 us
    pallas_call x1, Pallas kernels, on_device(): pl.pallas_call(gate_kernel, grid_spec=pltpu.PrefetchScalarGridSpec(num_sc...  14.4 us
    pallas_call x1, Pallas kernels, on_device(): pl.pallas_call(norm_kernel, grid=(chunks,), in_specs=[rows(width), pl.Blo...  9.91 us
    pallas_call x1, Pallas kernels, on_device(): pl.pallas_call(functools.partial(sum_kernel, n_head), in_specs=[vmem], ou...  7.58 us
    ppermute x1, starting transfers between devices, on_device(): prev_low = lax.ppermute(low_tail, 'seq', [(i, i + 1) for i in range(ends)])  5 us
    unnamed x20, local copies, waits for them, and re-layouts  4.4 us
  transfers between devices with their start and end apart: 2, of which 0 were waited for; matrix products, arithmetic and copies ran while one was open for 3% of the time, Pallas kernels for 0%

profile of v1, /device:TPU:1, one launch (start us, length us, event | category | flops | bytes accessed | tf_op | source)
XLA Modules:
  0.0 131.7 jit_solution(18082099790485173426)
XLA Ops:
  0.0 0.0 copy-start.6
  0.0 1.2 fusion.13
  1.2 0.8 fusion.10
  3.2 0.7 fusion.11
  4.0 1.3 collective-permute-start
  5.3 5.0 %collective-permute-start.1 = (bf16[8,2304]{1,0:T(8,128)(2,1)S(1)}, bf16[8,2304]{1,0:T(8,128)(2,1)S(1)}, u32[]{:S(2)}, u32[]{:S(2)}) collective-permute-start(bf16[8,2304]{1,0:T(8,128)(2,1)S(1)} %get-tuple-element.37), channel_id=1, source_target_pairs={{0,8},{8,16},{16,24},{24,32},{32,40},{40,48},{48,56},{56,64},{64,7... | collective-permute-start | bytes 110600 | tf_op jit(solution)/shard_map/ppermute | solution.py:278
  13.9 0.8 pad_dynamic-slice_fusion.1
  14.7 0.2 convert_reduce_fusion
  15.0 0.1 convert_bitcast_fusion
  15.0 0.1 fusion.6
  15.2 0.7 multiply_bitcast_fusion
  15.8 0.1 broadcast_bitcast_fusion
  15.9 0.1 reduce_or.9
  16.1 0.8 convert_multiply_fusion
  16.8 0.1 add_convert_fusion.flags.swapped
  16.9 0.1 slice.53
  17.0 0.1 copy.26.rate_ref
  17.1 0.7 copy.25.bias_ref
  17.8 0.1 slice.51
  17.9 0.1 broadcast_in_dim.16
  18.1 0.1 broadcast_in_dim.35
  18.2 0.1 stack.35.info_ref
  18.4 0.0 collective-permute-done
  18.4 0.0 collective-permute-done.1
  18.4 0.0 copy-start
  18.4 1.0 copy-done
  19.5 0.0 copy-start.1
  19.5 1.0 copy-done.1
  20.5 0.0 copy-start.2
  20.5 0.9 copy-done.2
  21.4 23.9 %local.1 = (bf16[2048,2048]{1,0:T(8,128)(2,1)}, bf16[2048,128]{1,0:T(8,128)(2,1)S(1)}, bf16[2048,128]{1,0:T(8,128)(2,1)S(1)}, f32[2048,128]{1,0:T(8,128)S(1)}, f...) custom-call(s32[9]{0:T(128)S(1)} %add_convert_fusion.flags.swapped, ...), custom_call_target="tpu_custom_call" | custom-call | tf_op jit(solution)/shard_map/local/pallas_call | solution.py:309
  45.3 37.9 %exchange.1.sin_ref = bf16[16,2,128,128]{3,2,1,0:T(8,128)(2,1)S(1)} custom-call(bf16[16,2,144,128]{3,2,1,0:T(8,128)(2,1)S(1)} %get-tuple-element.20.msg_ref), custom_call_target="tpu_custom_call" | custom-call | tf_op jit(solution)/shard_map/exchange/pallas_call | solution.py:345
  83.2 0.0 copy-done.6
  83.2 0.1 broadcast_in_dim.36
  83.3 15.3 %inner.1.y_ref = bf16[2048,2048]{1,0:T(8,128)(2,1)} custom-call(bf16[2048,2048]{1,0:T(8,128)(2,1)} %get-tuple-element.14.feat_ref, bf16[2048,128]{1,0:T(8,128)(2,1)S(1)} %get-tuple-element.15.wc_ref, bf16[2048,128]{1,0:T(8,128)(2,1)S(1)} %get-tuple-element.16.rc_ref, f32[2048,128]{1,0:T(8,128)S(1)} %get-tuple-element.17.cols_ref, ...), custom_call_target="tpu_custom_call" | custom-call | tf_op jit(solution)/shard_map/inner/pallas_call | solution.py:359
  98.5 0.0 copy-start.4
  98.5 14.4 %gate.1 = (bf16[2048,2048]{1,0:T(8,128)(2,1)}, f32[8,2,128]{2,1,0:T(2,128)S(1)}) custom-call(s32[9]{0:T(128)S(1)} %add_convert_fusion.flags.swapped, bf16[2048,2048]{1,0:T(8,128)(2,1)} %inner.1.y_ref, bf16[2048,2048]{1,0:T(8,128)(2,1)} %gate_ref.1, bf16[2048,128]{1,0:T(8,128)(2,1)S(1)} %get-tuple-element.16.rc_ref, ...), custom_call_target="tpu_custom_call" | custom-call | tf_op jit(solution)/shard_map/gate/pallas_call | solution.py:372
  112.9 0.0 copy-start.5
  112.9 0.6 copy-done.5
  113.5 7.6 %sum.1.scale_ref = f32[8,2,128]{2,1,0:T(2,128)} custom-call(f32[8,2,128]{2,1,0:T(2,128)} %copy-done.5), custom_call_target="tpu_custom_call" | custom-call | tf_op jit(solution)/shard_map/sum/pallas_call | solution.py:391
  121.1 0.0 copy-done.4
  121.1 0.0 copy-start.3
  121.1 0.7 copy-done.3
  121.8 9.9 %norm.1 = bf16[2048,2048]{1,0:T(8,128)(2,1)} custom-call(bf16[2048,2048]{1,0:T(8,128)(2,1)} %get-tuple-element.21.gated_ref, f32[8,2,128]{2,1,0:T(2,128)S(1)} %copy-done.3, f32[1,2048]{1,0:T(1,128)S(1)} %bitcast.33), custom_call_target="tpu_custom_call" | custom-call | tf_op jit(solution)/shard_map/norm/pallas_call | solution.py:401
  (20 shorter events, 0.2 us)
Async XLA Ops:
  0.0 83.2 %copy-start.6 = (f32[16]{0:T(128)S(1)}, f32[16]{0:T(128)}, u32[]{:S(2)}) copy-start(f32[16]{0:T(128)} %param.21) | copy-start | bytes 196
  4.0 14.4 %collective-permute-start = (bf16[8,2304]{1,0:T(8,128)(2,1)S(1)}, bf16[8,2304]{1,0:T(8,128)(2,1)S(1)}, u32[]{:S(2)}, u32[]{:S(2)}) collective-permute-start(bf16[8,2304]{1,0:T(8,128)(2,1)S(1)} %get-tuple-element.36), channel_id=1, source_target_pairs={{8,0},{16,8},{24,16},{32,24},{40,32},{48,40},{56,48},{64,56},{72,6... | collective-permute-start | bytes 110600 | tf_op jit(solution)/shard_map/ppermute | solution.py:279
  5.3 13.1 %collective-permute-start.1 = (bf16[8,2304]{1,0:T(8,128)(2,1)S(1)}, bf16[8,2304]{1,0:T(8,128)(2,1)S(1)}, u32[]{:S(2)}, u32[]{:S(2)}) collective-permute-start(bf16[8,2304]{1,0:T(8,128)(2,1)S(1)} %get-tuple-element.37), channel_id=1, source_target_pairs={{0,8},{8,16},{16,24},{24,32},{32,40},{40,48},{48,56},{56,64},{64,7... | collective-permute-start | bytes 110600 | tf_op jit(solution)/shard_map/ppermute | solution.py:278
  18.4 1.0 copy-start
  19.5 1.0 copy-start.1
  20.5 0.9 copy-start.2
  98.5 22.6 %copy-start.4 = (f32[2048]{0:T(1024)S(1)}, f32[2048]{0:T(1024)}, u32[]{:S(2)}) copy-start(f32[2048]{0:T(1024)} %param.25) | copy-start | bytes 24580
  112.9 0.6 copy-start.5
  121.1 0.7 copy-start.3

commit v2 on v0

v2 whole, which is shorter than its diff:
```python
import functools

import jax
import jax.numpy as jnp
from jax import lax
from jax.experimental import pallas as pl
from jax.experimental.pallas import tpu as pltpu
from jax.sharding import PartitionSpec as P

H = 128
P_SIZE = 128
N = 128
G = 8
Q = 256
SETS = 2
EPSILON = 1e-05
LOG2E = 1.4426950408889634
MESH = pl.DeviceIdType.MESH
MIB = 2**20
F32 = jnp.float32
BF16 = jnp.bfloat16
MESSAGE = N + 16
RIM = 16


def silu_of_half(h):
    return h + h * jnp.tanh(h)


def conv_tile(ext, taps, masks):
    total = ext[8:] * taps[3:4]
    for back in (1, 2, 3):
        total = total + pltpu.roll(ext, back, 0)[8:] * taps[3 - back : 4 - back] * masks[back - 1]
    return silu_of_half(total)


def spread_out(cols, lane, width=P_SIZE):
    return jnp.broadcast_to(cols[:, lane : lane + 1], (cols.shape[0], width))


def head_order(n, sets):
    if n == 16 and sets == 2:
        return [0, 2, 5, 7, 8, 10, 13, 15, 1, 3, 4, 6, 9, 11, 12, 14]
    return list(range(n))


def main_kernel(
    n_seq, n_head, comm, phases,
    x_hbm, gate_hbm, write_ref, read_ref, step_ref, bias_ref, rate_ref, info_ref, flip_ref, taps_ref, skip_ref,
    out_hbm, scale_ref,
    body, gate, wct, wc, rc, cols, brow, decay, half_decay, sloc, state, prev, carry,
    upper, scores, squares, sq, rim_mine, rim_in, msg, recv, back, entering, sums,
    x_sem, g_sem, o_sem, t_sem, h_send, h_recv, s1, r1, s2, r2, s3, r3,
):
    tokens, width = body.shape
    heads = width // P_SIZE
    chunks = tokens // Q
    per_half = chunks // 2
    half_rows = tokens // 2
    per_set = heads // SETS
    set_width = per_set * P_SIZE
    me = lax.axis_index("seq") if comm else 0
    my_head = lax.axis_index("head") if comm else 0
    device_of = head_order(n_seq, SETS)
    TAIL, CUM, ENTER, ENTER_HALF, INFO = (k * per_set for k in range(5))

    def rows_of(c):
        return pl.ds(pl.multiple_of(c * Q, Q), Q)

    def x_copy(c):
        return pltpu.make_async_copy(x_hbm.at[rows_of(c)], body.at[rows_of(c)], x_sem.at[c])

    def gate_copy(c):
        return pltpu.make_async_copy(gate_hbm.at[rows_of(c)], gate.at[rows_of(c)], g_sem.at[c])

    def out_copy(c):
        return pltpu.make_async_copy(body.at[rows_of(c)], out_hbm.at[rows_of(c)], o_sem.at[c])

    def tail_copy(k):
        end = half_rows * (k + 1)
        return pltpu.make_async_copy(
            x_hbm.at[pl.ds(end - RIM, RIM)], rim_in.at[k, :, pl.ds(0, width)], t_sem.at[k]
        )

    for k in (0, 1):
        tail_copy(k).start()
    for c in range(chunks):
        x_copy(c).start()
    for c in range(chunks):
        gate_copy(c).start()

    if comm:
        barrier = pltpu.get_barrier_semaphore()
        for k in range(1, n_seq):
            pl.semaphore_signal(barrier, inc=1, device_id={"seq": lax.rem(me + k, n_seq)}, device_id_type=MESH)
        for k in range(1, n_head):
            pl.semaphore_signal(barrier, inc=1, device_id={"head": lax.rem(my_head + k, n_head)}, device_id_type=MESH)

    flip = flip_ref[0:1, 0:1]

    def pick(second, here, there):
        return jnp.where(jnp.broadcast_to(second, here.shape) > 0.5, there, here)

    for k in (0, 1):
        tail_copy(k).wait()
        end = half_rows * (k + 1)
        rim_in[k, :, width : width + N] = write_ref[end - RIM : end]
        rim_in[k, :, width + N :] = read_ref[end - RIM : end]
    first, second = rim_in[0].astype(F32), rim_in[1].astype(F32)
    rim_mine[0] = pick(flip, first, second).astype(BF16)
    rim_mine[1] = pick(flip, second, first).astype(BF16)
    rim_copies = []
    if comm:
        pl.semaphore_wait(barrier, n_seq - 1 + n_head - 1)
        for k, to in ((0, lax.rem(me + 1, n_seq)), (1, lax.rem(me + n_seq - 1, n_seq))):
            rim_copies.append(
                pltpu.make_async_remote_copy(
                    src_ref=rim_mine.at[k], dst_ref=rim_in.at[2 + k], send_sem=h_send.at[k],
                    recv_sem=h_recv.at[k], device_id={"seq": to}, device_id_type=MESH,
                )
            )
            rim_copies[-1].start()

    row = lax.broadcasted_iota(jnp.int32, (Q, Q), 0)
    col = lax.broadcasted_iota(jnp.int32, (Q, Q), 1)
    upper[...] = jnp.where(row <= col, 1.0, 0.0).astype(F32)
    state[...] = jnp.zeros_like(state)

    def prepare(c, _):
        at = pl.ds(pl.multiple_of(c * Q, Q), Q)
        step = jax.nn.softplus(step_ref[:, at] + bias_ref[...])
        cum = jnp.dot(
            step * rate_ref[...], upper[...], precision=lax.Precision.HIGHEST, preferred_element_type=F32
        )
        info = info_ref[:, at]
        seg, before, before_half, seg_end = info[0:1], info[4:5], info[5:6], info[6:7]
        cum_end = cum[:, Q - 1 : Q]
        base = jnp.where(lax.rem(c, per_half) == 0, 0.0, carry[:, 0:1])
        tail = jnp.where(seg == seg_end, jnp.exp2(cum_end - cum) * step, 0.0)
        enter = jnp.where(seg == before, jnp.exp2(cum), 0.0)
        enter_half = jnp.where(seg == before_half, jnp.exp2(base + cum), 0.0)
        decay[c] = jnp.broadcast_to(enter[:, Q - 1 : Q], (heads, 128))
        half_decay[c] = jnp.broadcast_to(enter_half[:, Q - 1 : Q], (heads, 128))
        carry[...] = jnp.broadcast_to(base + cum_end, carry.shape)
        brow[c] = cum - jnp.log2(step)
        for g in range(SETS):
            own = slice(g * per_set, (g + 1) * per_set)
            fill = jnp.zeros((128 - 4 * per_set - 8, Q), F32)
            cols[g, rows_of(c)] = jnp.transpose(
                jnp.concatenate([tail[own], cum[own], enter[own], enter_half[own], info, fill], axis=0)
            )
        return 0

    if phases >= 1:
        lax.fori_loop(0, chunks, prepare, 0)

    if comm:
        for copy in rim_copies:
            copy.wait()
    low_in = rim_in[2, RIM - 8 :].astype(F32)
    high_in = rim_in[3, RIM - 8 :].astype(F32)
    if comm:
        high_in = jnp.where(me == n_seq - 1, rim_mine[0, RIM - 8 :].astype(F32), high_in)
    rims = (pick(flip, low_in, high_in), pick(flip, high_in, low_in))
    prev[0] = rims[0]
    prev[1] = rims[1]

    def masks_of(c):
        both = cols[0, rows_of(c)]
        return [spread_out(both, INFO + k) for k in (1, 2, 3)]

    def group_part(c, _):
        masks = masks_of(c)
        half = c // per_half

        def conv(ref, c0):
            cur = ref[rows_of(c)].astype(F32)
            ext = jnp.concatenate([prev[half, :, c0 : c0 + N], cur], axis=0)
            prev[half, :, c0 : c0 + N] = cur[Q - 8 :]
            return conv_tile(ext, taps_ref[:, c0 : c0 + N], masks)

        w = conv(write_ref, width)
        r = conv(read_ref, width + N)
        rc[rows_of(c)] = r.astype(BF16)
        wc[rows_of(c)] = w.astype(BF16)
        wct[c] = jnp.transpose(w).astype(BF16)
        return 0

    if phases >= 2:
        lax.fori_loop(0, chunks, group_part, 0)

    def local_part(k, _):
        g, c = k // chunks, lax.rem(k, chunks)
        half = c // per_half
        masks = masks_of(c)
        own = cols[g, rows_of(c)]

        @pl.when(g == 0)
        def _():
            x_copy(c).wait()

        for pair in range(per_set // 2):
            scaled = []
            at = pl.ds(pl.multiple_of(g * set_width + pair * 2 * P_SIZE, 2 * P_SIZE), 2 * P_SIZE)
            for j in (0, 1):
                h = 2 * pair + j
                one = pl.ds(pl.multiple_of(g * set_width + h * P_SIZE, P_SIZE), P_SIZE)
                cur = body[rows_of(c), one].astype(F32)
                ext = jnp.concatenate([prev[half, :, one], cur], axis=0)
                prev[half, :, one] = cur[Q - 8 :]
                feat = conv_tile(ext, taps_ref[:, one], masks).astype(BF16)
                body[rows_of(c), one] = feat
                scaled.append((feat.astype(F32) * spread_out(own, TAIL + h)).astype(BF16))
            add = jnp.dot(wct[c], jnp.concatenate(scaled, axis=1), preferred_element_type=F32)
            old = state[half, :, at]
            sloc[c, :, at] = old.astype(BF16)
            drow = [decay[c, pl.ds(g * per_set + 2 * pair + j, 1), :] for j in (0, 1)]
            state[half, :, at] = old * jnp.concatenate(drow, axis=1) + add
        return 0

    def send_states(g):
        for h in range(g * per_set, (g + 1) * per_set):
            at = slice(h * P_SIZE, (h + 1) * P_SIZE)
            first, second = state[0, :, at], state[1, :, at]
            msg[h, 0, :N] = pick(flip, first, second).astype(BF16)
            msg[h, 1, :N] = pick(flip, second, first).astype(BF16)
            dec = [jnp.broadcast_to(half_decay[k, h : h + 1], (8, 128)) for k in (per_half - 1, chunks - 1)]
            for k, whole in ((0, pick(flip, dec[0], dec[1])), (1, pick(flip, dec[1], dec[0]))):
                high = whole.astype(BF16).astype(F32)
                msg[h, k, N:] = jnp.concatenate([high, whole - high], axis=0).astype(BF16)
        if comm:
            for h in range(g * per_set, (g + 1) * per_set):
                to = device_of[h]

                @pl.when(me != to)
                def _():
                    state_copy(h).start()

                @pl.when(me == to)
                def _():
                    recv[me] = msg[h]

    def state_copy(h):
        return pltpu.make_async_remote_copy(
            src_ref=msg.at[h], dst_ref=recv.at[me], send_sem=s1.at[h], recv_sem=r1.at[me],
            device_id={"seq": device_of[h]}, device_id_type=MESH,
        )

    def state_arrival(src):
        return pltpu.make_async_remote_copy(
            src_ref=msg.at[0], dst_ref=recv.at[src], send_sem=s1.at[0], recv_sem=r1.at[src],
            device_id={"seq": src}, device_id_type=MESH,
        )

    def enter_copy(h, to):
        return pltpu.make_async_remote_copy(
            src_ref=back.at[to], dst_ref=entering.at[h], send_sem=s2.at[to], recv_sem=r2.at[h],
            device_id={"seq": to}, device_id_type=MESH,
        )

    def scan_states(g):
        if not comm:
            return
        for h in range(g * per_set, (g + 1) * per_set):
            @pl.when(me == device_of[h])
            def _():
                for src in range(n_seq):
                    @pl.when(me != src)
                    def _():
                        state_arrival(src).wait_recv()

                def advance(total, src, half):
                    back[src, half] = total.astype(BF16)
                    keep = recv[src, half, N : N + 1].astype(F32) + recv[src, half, N + 8 : N + 9].astype(F32)
                    return total * keep + recv[src, half, :N].astype(F32)

                total = lax.fori_loop(
                    0, n_seq, lambda k, t: advance(t, k, 0), jnp.zeros((N, P_SIZE), F32)
                )
                lax.fori_loop(0, n_seq, lambda k, t: advance(t, n_seq - 1 - k, 1), total)
                for to in range(n_seq):
                    if to != device_of[h]:
                        enter_copy(h, to).start()
                entering[h] = back[device_of[h]]

    if phases >= 3:
        for g in range(SETS):
            lax.fori_loop(g * chunks, (g + 1) * chunks, local_part, 0)
            send_states(g)

    def inner_part(k, _):
        g, c = k // chunks, lax.rem(k, chunks)
        own = cols[g, rows_of(c)]
        half = Q // 2

        @pl.when(g == 0)
        def _():
            gate_copy(c).wait()
            full = lax.dot_general(
                rc[rows_of(c)], wc[rows_of(c)], (((1,), (1,)), ((), ())), preferred_element_type=F32
            )
            seg_row = info_ref[0:1, pl.ds(pl.multiple_of(c * Q, Q), Q)]
            keep = (own[:, INFO : INFO + 1] == seg_row) & (col <= row)
            scores[c] = jnp.where(keep, full, 0.0)

        masked = scores[c]
        r = rc[rows_of(c)]
        for pair in range(per_set // 2):
            at = pl.ds(pl.multiple_of(g * set_width + pair * 2 * P_SIZE, 2 * P_SIZE), 2 * P_SIZE)
            inter = jnp.dot(r, sloc[c, :, at], preferred_element_type=F32)
            for j in (0, 1):
                h = 2 * pair + j
                one = pl.ds(pl.multiple_of(g * set_width + h * P_SIZE, P_SIZE), P_SIZE)
                feat = body[rows_of(c), one]
                cum = spread_out(own, CUM + h)
                bro = brow[c, pl.ds(g * per_set + h, 1), :]

                def tile(t, s):
                    spread = cum[t * half : (t + 1) * half] - bro[:, s * half : (s + 1) * half]
                    part = masked[t * half : (t + 1) * half, s * half : (s + 1) * half]
                    return (part * jnp.exp2(spread)).astype(BF16)

                top = jnp.dot(tile(0, 0), feat[:half], preferred_element_type=F32)
                low = jnp.dot(
                    jnp.concatenate([tile(1, 0), tile(1, 1)], axis=1), feat, preferred_element_type=F32
                )
                y = jnp.concatenate([top, low], axis=0)
                y = y + inter[:, j * P_SIZE : (j + 1) * P_SIZE] * spread_out(own, ENTER + h)
                y = y + feat.astype(F32) * skip_ref[:, one]
                sg = silu_of_half(gate[rows_of(c), one].astype(F32) * 0.5)
                gate[rows_of(c), one] = sg.astype(BF16)
                body[rows_of(c), one] = (y * sg).astype(BF16)
        return 0

    total_steps = SETS * chunks
    if phases >= 4:
        lax.fori_loop(0, 3, inner_part, 0)
        scan_states(0)
        lax.fori_loop(3, 12, inner_part, 0)
        scan_states(1)
        lax.fori_loop(12, total_steps, inner_part, 0)

    def finish_part(k, _):
        g, c = k // chunks, lax.rem(k, chunks)
        own = cols[g, rows_of(c)]
        r = rc[rows_of(c)]
        second = c >= per_half
        pick_high = jnp.where(second, 1.0 - flip, flip)
        total = jnp.where(g == 0, 0.0, squares[c])
        for pair in range(per_set // 2):
            states = []
            for j in (0, 1):
                h = g * per_set + 2 * pair + j
                low, high = entering[h, 0].astype(F32), entering[h, 1].astype(F32)
                states.append(pick(pick_high, low, high).astype(BF16))
            inter = jnp.dot(r, jnp.concatenate(states, axis=1), preferred_element_type=F32)
            for j in (0, 1):
                h = 2 * pair + j
                one = pl.ds(pl.multiple_of(g * set_width + h * P_SIZE, P_SIZE), P_SIZE)
                scaled = inter[:, j * P_SIZE : (j + 1) * P_SIZE] * spread_out(own, ENTER_HALF + h)
                gated = body[rows_of(c), one].astype(F32) + scaled * gate[rows_of(c), one].astype(F32)
                total = total + gated * gated
                body[rows_of(c), one] = gated.astype(BF16)
        squares[c] = total

        @pl.when(g == SETS - 1)
        def _():
            out_copy(c).start()
            sums_here = jnp.sum(jnp.transpose(total), axis=0, keepdims=True)
            sq[c] = jnp.concatenate([sums_here[:, :128], sums_here[:, 128:]], axis=0)

        return 0

    for g in range(SETS):
        if comm:
            for h in range(g * per_set, (g + 1) * per_set):
                @pl.when(me != device_of[h])
                def _():
                    enter_copy(h, device_of[h]).wait_recv()

        if phases >= 5:
            lax.fori_loop(g * chunks, (g + 1) * chunks, finish_part, 0)

    total = sq[...]
    if comm:
        copies = []
        for k in range(1, n_head):
            copies.append(
                pltpu.make_async_remote_copy(
                    src_ref=sq, dst_ref=sums.at[k], send_sem=s3.at[k], recv_sem=r3.at[k],
                    device_id={"head": lax.rem(my_head + k, n_head)}, device_id_type=MESH,
                )
            )
            copies[-1].start()
        for k in range(1, n_head):
            copies[k - 1].wait()
            total = total + sums[k]
        for h in range(heads):
            @pl.when(me != device_of[h])
            def _():
                state_copy(h).wait_send()
        for h in range(heads):
            @pl.when(me == device_of[h])
            def _():
                for to in range(n_seq):
                    if to != device_of[h]:
                        enter_copy(h, to).wait_send()
    scale_ref[...] = lax.rsqrt(total / (H * P_SIZE) + EPSILON)
    if phases >= 5:
        for c in range(chunks):
            out_copy(c).wait()
    if phases < 4:
        for c in range(chunks):
            gate_copy(c).wait()
    if phases < 3:
        for c in range(chunks):
            x_copy(c).wait()


def main_call(n_seq, n_head, comm, phases, inputs, gates, small):
    tokens, width = inputs.shape
    heads = width // P_SIZE
    chunks = tokens // Q
    wide = width + 2 * N
    vmem = pl.BlockSpec(memory_space=pltpu.VMEM)
    hbm = pl.BlockSpec(memory_space=pl.ANY)
    dma = lambda n: pltpu.SemaphoreType.DMA((n,))
    return pl.pallas_call(
        functools.partial(main_kernel, n_seq, n_head, comm, phases),
        in_specs=[hbm, hbm] + [vmem] * len(small),
        out_specs=[hbm, vmem],
        out_shape=[
            jax.ShapeDtypeStruct((tokens, width), BF16),
            jax.ShapeDtypeStruct((chunks, Q // 128, 128), F32),
        ],
        scratch_shapes=[
            pltpu.VMEM((tokens, width), BF16),
            pltpu.VMEM((tokens, width), BF16),
            pltpu.VMEM((chunks, N, Q), BF16),
            pltpu.VMEM((tokens, N), BF16),
            pltpu.VMEM((tokens, N), BF16),
            pltpu.VMEM((SETS, tokens, 128), F32),
            pltpu.VMEM((chunks, heads, Q), F32),
            pltpu.VMEM((chunks, heads, 128), F32),
            pltpu.VMEM((chunks, heads, 128), F32),
            pltpu.VMEM((chunks, N, width), BF16),
            pltpu.VMEM((2, N, width), F32),
            pltpu.VMEM((2, 8, wide), F32),
            pltpu.VMEM((heads, 128), F32),
            pltpu.VMEM((Q, Q), F32),
            pltpu.VMEM((chunks, Q, Q), F32),
            pltpu.VMEM((chunks, Q, P_SIZE), F32),
            pltpu.VMEM((chunks, Q // 128, 128), F32),
            pltpu.VMEM((2, RIM, wide), BF16),
            pltpu.VMEM((4, RIM, wide), BF16),
            pltpu.VMEM((heads, 2, MESSAGE, P_SIZE), BF16),
            pltpu.VMEM((n_seq, 2, MESSAGE, P_SIZE), BF16),
            pltpu.VMEM((n_seq, 2, N, P_SIZE), BF16),
            pltpu.VMEM((heads, 2, N, P_SIZE), BF16),
            pltpu.VMEM((n_head, chunks, Q // 128, 128), F32),
            dma(chunks), dma(chunks), dma(chunks), dma(2), dma(2), dma(2),
            dma(heads), dma(n_seq), dma(n_seq), dma(heads), dma(n_head), dma(n_head),
        ],
        compiler_params=pltpu.CompilerParams(
            vmem_limit_bytes=56 * MIB,
            **(dict(collective_id=0, has_side_effects=True) if comm else {}),
        ),
        name="main",
    )(inputs, gates, *small)


def norm_kernel(gated_ref, scale_ref, gain_ref, out_ref):
    for k in range(scale_ref.shape[0]):
        scale = scale_ref[k]
        row = jnp.concatenate([scale[0:1], scale[1:2]], axis=1)
        col = jnp.transpose(jnp.broadcast_to(row, (128, Q)))
        at = slice(k * Q, (k + 1) * Q)
        for c in range(gated_ref.shape[1] // 128):
            c0, c1 = c * 128, (c + 1) * 128
            out_ref[at, c0:c1] = (gated_ref[at, c0:c1].astype(F32) * col * gain_ref[:, c0:c1]).astype(BF16)


def norm_call(gated, scale, gain):
    tokens, width = gated.shape
    block = 2 * Q
    rows = pl.BlockSpec((block, width), lambda i: (i, 0))
    return pl.pallas_call(
        norm_kernel,
        grid=(tokens // block,),
        in_specs=[
            rows, pl.BlockSpec((block // Q, Q // 128, 128), lambda i: (i, 0, 0)),
            pl.BlockSpec((1, width), lambda i: (0, 0)),
        ],
        out_specs=rows,
        out_shape=jax.ShapeDtypeStruct((tokens, width), BF16),
        compiler_params=pltpu.CompilerParams(vmem_limit_bytes=32 * MIB),
        name="norm",
    )(gated, scale, gain)


def on_device(
    inputs, gates, writes, reads, step_raw, step_bias, decay_rate, skip_gain,
    conv_inputs, conv_writes, conv_reads, norm_gain, positions, segments,
    comm=True, phases=5,
):
    tokens, width = inputs.shape
    half_rows = tokens // 2
    chunks = tokens // Q
    per_half = chunks // 2
    n_seq = lax.axis_size("seq") if comm else 16
    n_head = lax.axis_size("head") if comm else 8
    first_start, second_start = positions[0], positions[half_rows]
    swapped = first_start > second_start

    seg_padded = jnp.concatenate([jnp.full((3,), -1, jnp.int32), segments])
    windows = jnp.stack(
        [lax.dynamic_slice_in_dim(seg_padded, s, half_rows + 3) for s in (first_start, second_start)]
    )
    seg = windows[:, 3:]
    same = [seg == windows[:, 3 - k : 3 - k + half_rows] for k in (1, 2, 3)]
    before = jnp.broadcast_to(windows[:, 2 : 2 + half_rows : Q, None], (2, per_half, Q))
    seg_end = jnp.broadcast_to(seg[:, Q - 1 :: Q, None], (2, per_half, Q))
    before_half = jnp.broadcast_to(windows[:, 2:3], (2, half_rows))
    info = jnp.stack(
        [a.reshape(tokens).astype(F32) for a in (seg, *same, before, before_half, seg_end, jnp.zeros_like(seg))]
    )
    flip = jnp.broadcast_to(swapped.astype(F32), (8, 128))
    taps = jnp.concatenate([conv_inputs, conv_writes, conv_reads], axis=1).astype(F32) * 0.5
    small = (
        writes, reads, step_raw, step_bias[:, None], -LOG2E * decay_rate[:, None], info, flip, taps,
        jnp.repeat(skip_gain, P_SIZE)[None],
    )
    gated, scale = main_call(n_seq, n_head, comm, phases, inputs, gates, small)
    return norm_call(gated, scale, norm_gain[None])


def solution(mesh):
    return jax.shard_map(
        on_device,
        mesh=mesh,
        in_specs=(
            P("seq", "head"), P("seq", "head"), P("seq", "head"), P("seq", "head"), P("head", "seq"),
            P("head"), P("head"), P("head"), P(None, "head"), P(None, "head"), P(None, "head"),
            P("head"), P("seq"), P(),
        ),
        out_specs=P("seq", "head"),
        check_vma=False,
    )
```

time: 673 us -> 111 us (0.16)
  waiting for transfers between devices: 193 us -> 0 us
  local copies, waits for them, and re-layouts: 182 us -> 11.2 us
  other arithmetic: 153 us -> 2.44 us
  Pallas kernels: 0 us -> 92.1 us
  matrix products: 61.2 us -> 0 us
  blocking collectives: 47.9 us -> 0 us
  between operations: 19.3 us -> 4.95 us
  loops' own time: 6.75 us -> 0 us
    all_gather x2 -> x0, waiting for transfers between devices: 192 us -> none  [carried_in(): everything = jax.tree.map(lambda part: lax.all_gather(part, axis), x)]
    pallas_call x0 -> x2, Pallas kernels: none -> 92.1 us  [the longest x1 87.5 us: main_call(): pl.pallas_call(functools.partial(main_kernel, n_seq, n_head, comm, phases...]
    dynamic_update_slice x24 -> x0, local copies, waits for them, and re-layouts: 86.4 us -> none  [on_device(): lax.map(lambda a: block_parts(*a), (feature_blocks, write_blocks, read_bl...]
    dot_general x16 -> x0, matrix products: 61.2 us -> none  [the longest x4 33.9 us: block_parts(): jnp.einsum('gets,sgep->tgep', weights, features, preferred_element_type=j...]
    select_n x64 -> x0, other arithmetic: 60.4 us -> none  [the longest x48 53.7 us: lap(): return jax.tree.map(lambda a, b: jnp.where(reached, a, b), new, before)]
    convert_element_type x11 -> x3, other arithmetic: 48.6 us -> 0.2 us  [on_device(): a.reshape(tokens).astype(F32)]
    dynamic_slice x33 -> x1, local copies, waits for them, and re-layouts: 39.7 us -> 0.8 us  [on_device(): lax.dynamic_slice_in_dim(seg_padded, s, half_rows + 3)]
    all_gather x2 -> x0, blocking collectives: 35.2 us -> none  [carried_in(): everything = jax.tree.map(lambda part: lax.all_gather(part, axis), x)]
  transfers between devices with their start and end apart: 4 -> 0, of which waited for: 2 -> 0; matrix products, arithmetic and copies ran while one was open for 2% -> 0% of each run, Pallas kernels for 0% -> 0%
where the time goes in v2:
time: 111 us
  Pallas kernels  92.1 us (83%)
  local copies, waits for them, and re-layouts  11.2 us (10%)
  between operations  4.95 us (4%)
  other arithmetic  2.44 us (2%)
    pallas_call x1, Pallas kernels, main_call(): pl.pallas_call(functools.partial(main_kernel, n_seq, n_head, comm, phases...  87.5 us
    pallas_call x1, Pallas kernels, norm_call(): pl.pallas_call(norm_kernel, grid=(tokens // block,), in_specs=[rows, pl.B...  4.54 us
    unnamed x12, local copies, waits for them, and re-layouts  4.2 us

profile of v2, /device:TPU:1, one launch (start us, length us, event | category | flops | bytes accessed | tf_op | source)
XLA Modules:
  0.0 110.7 jit_solution(8898219115984039600)
XLA Ops:
  0.0 0.7 multiply_bitcast_fusion
  0.7 1.2 %fusion.9 = (s32[1]{0:T(128)}, s32[1]{0:T(128)}) fusion(s32[2048]{0:T(1024)} %param.26), kind=kLoop, calls=%fused_computation.29 | loop fusion | bytes 16 | tf_op jit(solution)/shard_map/slice | solution.py:512
  6.7 0.6 broadcast_in_dim.34.flip_ref
  7.3 0.7 copy.26.rate_ref
  8.0 1.3 %copy.25.bias_ref = f32[16,1]{1,0:T(8,128)} copy(f32[16,1]{0,1:T(1,128)} %bitcast.34) | data formatting | bytes 128 | tf_op jit(solution)/shard_map/broadcast_in_dim | solution.py:530
  9.3 1.3 %broadcast_in_dim.35 = f32[16,128]{1,0:T(8,128)} broadcast(f32[16]{0:T(128)} %param.21), dimensions={0} | broadcast | bytes 8256 | tf_op jit(solution)/shard_map/broadcast_in_dim | solution.py:531
  10.6 0.8 pad_dynamic-slice_fusion.1
  11.4 0.2 convert_reduce_fusion
  11.6 0.1 broadcast_bitcast_fusion
  11.7 0.1 slice.33
  11.8 0.1 broadcast_in_dim.15
  11.9 0.1 fusion.6
  12.0 0.1 slice.35
  12.1 0.1 broadcast_in_dim.33
  12.2 0.1 fusion.5
  12.4 0.7 stack.26.info_ref
  13.2 1.4 %convert_multiply_fusion.taps_ref = f32[4,2304]{1,0:T(4,128)} fusion(bf16[4,128]{1,0:T(4,128)(2,1)} %param.24, bf16[4,128]{1,0:T(4,128)(2,1)} %param.23, bf16[4,2048]{1,0:T(4,128)(2,1)} %param.22), kind=kLoop, calls=%fused_computation.2 | loop fusion | flops 64512 | bytes 55296 | tf_op jit(solution)/shard_map/mul | solution.py:528
  14.5 0.0 copy-start.1
  14.5 87.5 %main.1 = (bf16[2048,2048]{1,0:T(8,128)(2,1)}, f32[8,2,128]{2,1,0:T(2,128)}) custom-call(bf16[2048,2048]{1,0:T(8,128)(2,1)} %x_hbm.1, bf16[2048,2048]{1,0:T(8,128)(2,1)} %gate_hbm.1, bf16[2048,128]{1,0:T(8,128)(2,1)} %write_ref.1, bf16[2048,128]{1,0:T(8,128)(2,1)} %read_ref.1, f32[16,2048]{1,0:T(8,128)} %step_ref.1, f32[16,1]{1,0:T(8,128)} %copy.25.bias_ref, ...), custom_call_target="tpu_custom_call" | custom-call | tf_op jit(solution)/shard_map/main/pallas_call | solution.py:428
  102.1 0.0 copy-done.1
  102.1 0.0 copy-start
  102.1 3.4 %copy-done = bf16[2048,2048]{1,0:T(8,128)(2,1)S(1)} copy-done((bf16[2048,2048]{1,0:T(8,128)(2,1)S(1)}, bf16[2048,2048]{1,0:T(8,128)(2,1)}, u32[]{:S(2)}) %copy-start) | copy-done | bytes 8388632
  105.5 0.0 copy-start.2
  105.5 0.7 copy-done.2
  106.2 4.5 %norm.1 = bf16[2048,2048]{1,0:T(8,128)(2,1)} custom-call(bf16[2048,2048]{1,0:T(8,128)(2,1)S(1)} %copy-done, f32[8,2,128]{2,1,0:T(2,128)S(1)} %copy-done.2, f32[1,2048]{1,0:T(1,128)S(1)} %bitcast.27), custom_call_target="tpu_custom_call" | custom-call | tf_op jit(solution)/shard_map/norm/pallas_call | solution.py:487
  (14 shorter events, 0.1 us)
Async XLA Ops:
  14.5 87.6 %copy-start.1 = (f32[2048]{0:T(1024)S(1)}, f32[2048]{0:T(1024)}, u32[]{:S(2)}) copy-start(f32[2048]{0:T(1024)} %param.25) | copy-start | bytes 24580
  102.1 3.4 %copy-start = (bf16[2048,2048]{1,0:T(8,128)(2,1)S(1)}, bf16[2048,2048]{1,0:T(8,128)(2,1)}, u32[]{:S(2)}) copy-start(bf16[2048,2048]{1,0:T(8,128)(2,1)} %get-tuple-element.7.gated_ref) | copy-start | bytes 25165828
  105.5 0.7 copy-start.2

commit v3 on v2

v3 whole, which is shorter than its diff:
```python
import functools

import jax
import jax.numpy as jnp
from jax import lax
from jax.experimental import pallas as pl
from jax.experimental.pallas import tpu as pltpu
from jax.sharding import PartitionSpec as P

H = 128
P_SIZE = 128
N = 128
G = 8
Q = 256
SETS = 2
SCAN_AT = (4, 12)
VMEM_MAIN = 52
EPSILON = 1e-05
LOG2E = 1.4426950408889634
MESH = pl.DeviceIdType.MESH
MIB = 2**20
F32 = jnp.float32
BF16 = jnp.bfloat16
MESSAGE = N + 16
RIM = 16


def silu_of_half(h):
    return h + h * jnp.tanh(h)


def spread_out(cols, lane, width=P_SIZE):
    return jnp.broadcast_to(cols[:, lane : lane + 1], (cols.shape[0], width))


def scan_device(h, n):
    side = 4 if n == 16 else 1
    per_set = n // SETS
    g, j = h // per_set, h % per_set
    per_row = per_set // side
    y = j // per_row
    return y * (n // side) + (j % per_row) * SETS + (g - y) % SETS


def scan_head(me, n):
    side = 4 if n == 16 else 1
    per_row = n // SETS // side
    y, z = me // (n // side), lax.rem(me, n // side)
    g = lax.rem(y + z, SETS)
    return g, g * (n // SETS) + y * per_row + z // SETS


def main_kernel(
    n_seq, n_head, comm, phases,
    x_hbm, gate_hbm, write_ref, read_ref, step_ref, bias_ref, rate_ref, skip_ref, ci_ref, cw_ref, cr_ref,
    seg_ref, pos_ref,
    out_hbm, scale_ref,
    raw, feats, gate, wct, r_enter, r_half, cols, frow, trow, segs, decay, half_decay, loc_scale, half_scale,
    sloc, state, raw_group, taps, skips, shifts, upper, scores, squares, sq, rim_own, rim_mine, rim_in,
    msg, recv, back, entering, sums,
    x_sem, g_sem, o_sem, t_sem, h_send, h_recv, s1, r1, s2, r2, s3, r3,
):
    tokens, width = feats.shape
    heads = width // P_SIZE
    chunks = tokens // Q
    per_half = chunks // 2
    half_rows = tokens // 2
    per_set = heads // SETS
    set_width = per_set * P_SIZE
    side = Q // 2
    me = lax.axis_index("seq") if comm else 0
    my_head = lax.axis_index("head") if comm else 0
    my_set, my_scan = scan_head(me, n_seq)
    device_of = [scan_device(h, n_seq) for h in range(heads)]
    CUM, INFO = 0, heads
    first, second = pos_ref[0], pos_ref[half_rows]
    flip = jnp.where(first > second, 1, 0)

    def rows_of(c):
        return pl.ds(pl.multiple_of(c * Q, Q), Q)

    def lanes_of(start, count):
        return pl.ds(pl.multiple_of(start, P_SIZE), count)

    def window_of(c, rim):
        start = c * Q + (c // per_half) * RIM
        return pl.ds(pl.multiple_of(start if rim else start + RIM, RIM), Q + RIM if rim else Q)

    def x_copy(c):
        return pltpu.make_async_copy(x_hbm.at[rows_of(c)], raw.at[window_of(c, False)], x_sem.at[c])

    def gate_copy(c):
        return pltpu.make_async_copy(gate_hbm.at[rows_of(c)], gate.at[rows_of(c)], g_sem.at[c])

    def out_copy(c):
        return pltpu.make_async_copy(feats.at[rows_of(c)], out_hbm.at[rows_of(c)], o_sem.at[c])

    def tail_copy(k):
        end = half_rows * (k + 1)
        return pltpu.make_async_copy(
            x_hbm.at[pl.ds(end - RIM, RIM)], rim_own.at[k, :, pl.ds(0, width)], t_sem.at[k]
        )

    for k in (0, 1):
        tail_copy(k).start()
    for c in range(chunks):
        x_copy(c).start()
    for c in range(chunks):
        gate_copy(c).start()

    if comm:
        barrier = pltpu.get_barrier_semaphore()
        for k in range(1, n_seq):
            pl.semaphore_signal(barrier, inc=1, device_id={"seq": lax.rem(me + k, n_seq)}, device_id_type=MESH)
        for k in range(1, n_head):
            pl.semaphore_signal(barrier, inc=1, device_id={"head": lax.rem(my_head + k, n_head)}, device_id_type=MESH)

    for k in (0, 1):
        tail_copy(k).wait()
        end = half_rows * (k + 1)
        rim_own[k, :, width : width + N] = write_ref[end - RIM : end]
        rim_own[k, :, width + N :] = read_ref[end - RIM : end]
    rim_mine[0] = rim_own[flip]
    rim_mine[1] = rim_own[1 - flip]
    rim_copies = []
    if comm:
        pl.semaphore_wait(barrier, n_seq - 1 + n_head - 1)
        for k, to in ((0, lax.rem(me + 1, n_seq)), (1, lax.rem(me + n_seq - 1, n_seq))):
            rim_copies.append(
                pltpu.make_async_remote_copy(
                    src_ref=rim_mine.at[k], dst_ref=rim_in.at[k], send_sem=h_send.at[k],
                    recv_sem=h_recv.at[k], device_id={"seq": to}, device_id_type=MESH,
                )
            )
            rim_copies[-1].start()

    taps[:, :width] = ci_ref[...].astype(F32) * 0.5
    taps[:, width : width + N] = cw_ref[...].astype(F32) * 0.5
    taps[:, width + N :] = cr_ref[...].astype(F32) * 0.5
    state[...] = jnp.zeros_like(state)
    eye = lax.broadcasted_iota(jnp.int32, (heads, heads), 0) == lax.broadcasted_iota(jnp.int32, (heads, heads), 1)

    def column(ref):
        return jnp.sum(jnp.where(eye, jnp.broadcast_to(ref[...], (heads, heads)), 0.0), axis=1, keepdims=True)

    bias, rate = column(bias_ref), column(rate_ref) * -LOG2E
    skips[...] = jnp.broadcast_to(column(skip_ref), (heads, P_SIZE))
    lane = lax.broadcasted_iota(jnp.int32, (1, half_rows), 1)
    for k, start in ((0, first), (1, second)):
        at = start // half_rows

        def in_a_row(block):
            return jnp.concatenate([block[j : j + 1] for j in range(half_rows // 128)], axis=1).astype(F32)

        here = in_a_row(seg_ref[at])
        ahead = in_a_row(seg_ref[jnp.maximum(at - 1, 0)])
        ahead = jnp.where(jnp.full(ahead.shape, at, jnp.int32) > 0, ahead, -1.0)
        lines = [here]
        for ago in (1, 2, 3):
            lines.append(jnp.where(lane < ago, pltpu.roll(ahead, ago, 1), pltpu.roll(here, ago, 1)))
        for j, line in enumerate(lines):
            segs[j : j + 1, k * half_rows : (k + 1) * half_rows] = line

    row = lax.broadcasted_iota(jnp.int32, (Q, Q), 0)
    col = lax.broadcasted_iota(jnp.int32, (Q, Q), 1)
    upper[...] = jnp.where(row <= col, 1.0, 0.0).astype(F32)

    def by_chunk(one_of):
        return jnp.concatenate([one_of(c) for c in range(chunks)], axis=0)

    def chunk_lanes(c):
        return slice(c * Q, (c + 1) * Q)

    def prepare():
        raw_step = by_chunk(lambda c: step_ref[:, chunk_lanes(c)])
        step = jax.nn.softplus(raw_step + by_chunk(lambda c: bias))
        cum = jnp.dot(
            step * by_chunk(lambda c: rate), upper[...], precision=lax.Precision.HIGHEST, preferred_element_type=F32
        )
        cum_end = cum[:, Q - 1 : Q]
        middle = 0.5 * cum_end
        grown = jnp.exp2(cum - middle)
        factor = jnp.exp2(middle - cum) * step
        tail = jnp.exp2(cum_end - cum) * step
        wide = (heads, 128)
        for c in range(chunks):
            own = slice(c * heads, (c + 1) * heads)
            at = chunk_lanes(c)
            seg, one_ago = segs[0:1, at], segs[1:2, at]
            half_start = (c // per_half) * half_rows
            same = [jnp.where(seg == segs[k : k + 1, at], 1.0, 0.0) for k in (1, 2, 3)]
            enters = jnp.where(seg == one_ago[:, 0:1], 1.0, 0.0)
            enters_half = jnp.where(seg == segs[1:2, half_start : half_start + 1], 1.0, 0.0)
            leaves = jnp.where(seg == seg[:, Q - 1 : Q], 1.0, 0.0)
            base = jnp.zeros((heads, 1), F32) if c % per_half == 0 else base + end
            end, mid = cum_end[own], middle[own]
            frow[c] = factor[own]
            trow[c] = tail[own] * leaves
            decay[c] = jnp.broadcast_to(jnp.exp2(end) * enters[:, Q - 1 : Q], wide)
            half_decay[c] = jnp.broadcast_to(jnp.exp2(base + end) * enters_half[:, Q - 1 : Q], wide)
            loc_scale[c] = jnp.broadcast_to(jnp.exp2(mid), wide)
            half_scale[c] = jnp.broadcast_to(jnp.exp2(base + mid), wide)
            fill = jnp.zeros((128 - heads - 6, Q), F32)
            cols[c * Q : (c + 1) * Q] = jnp.transpose(
                jnp.concatenate([grown[own], seg, *same, enters, enters_half, fill], axis=0)
            )

    if phases >= 1:
        prepare()

    if comm:
        for copy in rim_copies:
            copy.wait()
        rim_in[1] = jnp.where(
            jnp.full(rim_in.shape[1:], me) == n_seq - 1, rim_mine[0].astype(F32), rim_in[1].astype(F32)
        ).astype(BF16)
    for k, rim in ((0, rim_in[flip]), (1, rim_in[1 - flip])):
        start = k * (half_rows + RIM)
        raw[start : start + RIM] = rim[:, :width]
        raw_group[start : start + RIM] = rim[:, width:]
        for j, ref in ((0, write_ref), (1, read_ref)):
            raw_group[start + RIM : start + RIM + half_rows, j * N : (j + 1) * N] = ref[
                k * half_rows : (k + 1) * half_rows
            ]

    to_row = lax.broadcasted_iota(jnp.int32, (side, RIM + side), 0)
    from_row = lax.broadcasted_iota(jnp.int32, (side, RIM + side), 1)

    def conv(source, c, lanes, tap_lanes):
        tap = [taps[k : k + 1, tap_lanes] for k in range(4)]
        x = source[window_of(c, True), lanes]
        out = []
        for b in (0, 1):
            moved = jnp.dot(shifts[2 * c + b], x[b * side : RIM + (b + 1) * side], preferred_element_type=F32)
            total = x[RIM + b * side : RIM + (b + 1) * side].astype(F32) * tap[3]
            for k in (1, 2, 3):
                total = total + moved[(k - 1) * side : k * side] * tap[3 - k]
            out.append(silu_of_half(total))
        return jnp.concatenate(out, axis=0)

    def group_part(c, _):
        info = cols[rows_of(c)]
        for b in (0, 1):
            for k in (1, 2, 3):
                same = spread_out(info[b * side : (b + 1) * side], INFO + k, RIM + side)
                hit = jnp.where(from_row == to_row + (RIM - k), same, 0.0)
                shifts[2 * c + b, (k - 1) * side : k * side] = hit.astype(BF16)
        both = conv(raw_group, c, slice(0, 2 * N), slice(width, width + 2 * N))
        w, r = both[:, :N], both[:, N:]
        wct[c] = jnp.transpose(w.astype(BF16).astype(F32))
        w, r = w.astype(BF16), r.astype(BF16)
        wide = r.astype(F32)
        r_enter[rows_of(c)] = (wide * spread_out(info, INFO + 4)).astype(BF16)
        r_half[rows_of(c)] = (wide * spread_out(info, INFO + 5)).astype(BF16)
        full = lax.dot_general(r, w, (((1,), (1,)), ((), ())), preferred_element_type=F32)
        seg_row = segs[0:1, lanes_of(c * Q, Q)]
        keep = (info[:, INFO : INFO + 1] == seg_row) & (col <= row)
        scores[c] = jnp.where(keep, full, 0.0)
        return 0

    if phases >= 2:
        lax.fori_loop(0, chunks, group_part, 0)

    def conv_part(g, c, _):
        if g == 0:
            x_copy(c).wait()
        for pair in range(per_set // 2):
            start = g * set_width + pair * 2 * P_SIZE
            at = slice(start, start + 2 * P_SIZE)
            feats[rows_of(c), at] = conv(raw, c, at, at).astype(BF16)
        return 0

    def state_part(g, c, _):
        half = c // per_half
        w = wct[c]
        for h in range(g * per_set, (g + 1) * per_set):
            one = slice(h, h + 1)
            scaled = (w * trow[c, one, :]).astype(BF16)
            add = jnp.dot(scaled, feats[rows_of(c), h * P_SIZE : (h + 1) * P_SIZE], preferred_element_type=F32)
            old = state[half, h]
            sloc[c, h] = (old * loc_scale[c, one, :]).astype(BF16)
            state[half, h] = old * decay[c, one, :] + add
        return 0

    def state_copy(h):
        return pltpu.make_async_remote_copy(
            src_ref=msg.at[h], dst_ref=recv.at[me], send_sem=s1.at[h], recv_sem=r1.at[me],
            device_id={"seq": device_of[h]}, device_id_type=MESH,
        )

    def state_arrival(src):
        return pltpu.make_async_remote_copy(
            src_ref=msg.at[0], dst_ref=recv.at[src], send_sem=s1.at[0], recv_sem=r1.at[src],
            device_id={"seq": src}, device_id_type=MESH,
        )

    def enter_copy(g, h, to):
        return pltpu.make_async_remote_copy(
            src_ref=back.at[to], dst_ref=entering[g].at[h - g * per_set], send_sem=s2.at[to], recv_sem=r2.at[h],
            device_id={"seq": to}, device_id_type=MESH,
        )

    def send_states(g):
        for h in range(g * per_set, (g + 1) * per_set):
            for k, half in ((0, flip), (1, 1 - flip)):
                msg[h, k, :N] = state[half, h].astype(BF16)
                whole = jnp.broadcast_to(half_decay[(half + 1) * per_half - 1, h : h + 1], (8, 128))
                high = whole.astype(BF16).astype(F32)
                msg[h, k, N:] = jnp.concatenate([high, whole - high], axis=0).astype(BF16)
            if comm:
                to = device_of[h]

                @pl.when(me != to)
                def _():
                    state_copy(h).start()

                @pl.when(me == to)
                def _():
                    recv[me] = msg[h]

    def scan_states(g):
        if not comm:
            return

        @pl.when(my_set == g)
        def _():
            for k in range(1, n_seq):
                state_arrival(lax.rem(me + k, n_seq)).wait_recv()

            def advance(total, src, half):
                back[src, half] = total.astype(BF16)
                keep = recv[src, half, N : N + 1].astype(F32) + recv[src, half, N + 8 : N + 9].astype(F32)
                return total * keep + recv[src, half, :N].astype(F32)

            total = lax.fori_loop(0, n_seq, lambda k, t: advance(t, k, 0), jnp.zeros((N, P_SIZE), F32))
            lax.fori_loop(0, n_seq, lambda k, t: advance(t, n_seq - 1 - k, 1), total)
            for k in range(1, n_seq):
                enter_copy(g, my_scan, lax.rem(me + k, n_seq)).start()
            entering[g][my_scan - g * per_set] = back[me]

    if phases >= 3:
        for g in range(SETS):
            lax.fori_loop(0, chunks, functools.partial(conv_part, g), 0)
            lax.fori_loop(0, chunks, functools.partial(state_part, g), 0)
            send_states(g)

    def inner_part(g, c, _):
        info = cols[rows_of(c)]
        if g == 0:
            gate_copy(c).wait()

        masked = scores[c]
        r = r_enter[rows_of(c)]
        for j in range(per_set):
            h = g * per_set + j
            one = slice(h * P_SIZE, (h + 1) * P_SIZE)
            feat = feats[rows_of(c), one]
            fac = frow[c, h : h + 1, :]
            top = jnp.concatenate([r[:side], (masked[:side, :side] * fac[:, :side]).astype(BF16)], axis=1)
            low = jnp.concatenate([r[side:], (masked[side:] * fac).astype(BF16)], axis=1)
            entry = sloc[c, h]
            y = jnp.concatenate(
                [
                    jnp.dot(top, jnp.concatenate([entry, feat[:side]], axis=0), preferred_element_type=F32),
                    jnp.dot(low, jnp.concatenate([entry, feat], axis=0), preferred_element_type=F32),
                ],
                axis=0,
            )
            grown = spread_out(info, CUM + h)
            opened = silu_of_half(gate[rows_of(c), one].astype(F32) * 0.5)
            y = (y * grown + feat.astype(F32) * skips[h : h + 1, :]) * opened
            gate[rows_of(c), one] = (grown * opened).astype(BF16)
            raw[rows_of(c), one] = y.astype(BF16)
        return 0

    def inner_steps(start, stop):
        for g in range(SETS):
            begin, end = max(start - g * chunks, 0), min(stop - g * chunks, chunks)
            if begin < end:
                lax.fori_loop(begin, end, functools.partial(inner_part, g), 0)

    if phases >= 4:
        done = 0
        for g, until in enumerate(SCAN_AT):
            inner_steps(done, until)
            scan_states(g)
            done = until
        inner_steps(done, SETS * chunks)

    def finish_part(g, c, _):
        r = r_half[rows_of(c)]
        which = jnp.where(c >= per_half, 1 - flip, flip)
        total = jnp.zeros((Q, P_SIZE), F32) if g == 0 else squares[c]
        for pair in range(per_set // 2):
            states = []
            for j in (0, 1):
                h = g * per_set + 2 * pair + j
                states.append((entering[g][2 * pair + j, which].astype(F32) * half_scale[c, h : h + 1, :]).astype(BF16))
            inter = jnp.dot(r, jnp.concatenate(states, axis=1), preferred_element_type=F32)
            for j in (0, 1):
                start = g * set_width + (2 * pair + j) * P_SIZE
                one = slice(start, start + P_SIZE)
                gated = raw[rows_of(c), one].astype(F32)
                gated = gated + inter[:, j * P_SIZE : (j + 1) * P_SIZE] * gate[rows_of(c), one].astype(F32)
                total = total + gated * gated
                feats[rows_of(c), one] = gated.astype(BF16)
        if g < SETS - 1:
            squares[c] = total
        else:
            out_copy(c).start()
            sums_here = jnp.sum(jnp.transpose(total), axis=0, keepdims=True)
            sq[c] = jnp.concatenate([sums_here[:, :128], sums_here[:, 128:]], axis=0)

        return 0

    for g in range(SETS):
        if comm:
            for h in range(g * per_set, (g + 1) * per_set):
                @pl.when(me != device_of[h])
                def _():
                    enter_copy(g, h, device_of[h]).wait_recv()

        if phases >= 5:
            lax.fori_loop(0, chunks, functools.partial(finish_part, g), 0)

    total = sq[...]
    if comm:
        copies = []
        for k in range(1, n_head):
            copies.append(
                pltpu.make_async_remote_copy(
                    src_ref=sq, dst_ref=sums.at[k], send_sem=s3.at[k], recv_sem=r3.at[k],
                    device_id={"head": lax.rem(my_head + k, n_head)}, device_id_type=MESH,
                )
            )
            copies[-1].start()
        for h in range(heads):
            @pl.when(me != device_of[h])
            def _():
                state_copy(h).wait_send()
        for k in range(1, n_seq):
            enter_copy(0, 0, lax.rem(me + k, n_seq)).wait_send()
        for k in range(1, n_head):
            copies[k - 1].wait()
            total = total + sums[k]
    scale_ref[...] = lax.rsqrt(total / (H * P_SIZE) + EPSILON)
    if phases >= 5:
        for c in range(chunks):
            out_copy(c).wait()
    if phases < 4:
        for c in range(chunks):
            gate_copy(c).wait()
    if phases < 3:
        for c in range(chunks):
            x_copy(c).wait()


def main_call(n_seq, n_head, comm, phases, inputs, gates, small, positions):
    tokens, width = inputs.shape
    heads = width // P_SIZE
    chunks = tokens // Q
    wide = width + 2 * N
    vmem = pl.BlockSpec(memory_space=pltpu.VMEM)
    hbm = pl.BlockSpec(memory_space=pl.ANY)
    dma = lambda n: pltpu.SemaphoreType.DMA((n,))
    return pl.pallas_call(
        functools.partial(main_kernel, n_seq, n_head, comm, phases),
        in_specs=[hbm, hbm] + [vmem] * len(small) + [pl.BlockSpec(memory_space=pltpu.SMEM)],
        out_specs=[hbm, vmem],
        out_shape=[
            jax.ShapeDtypeStruct((tokens, width), BF16),
            jax.ShapeDtypeStruct((chunks, Q // 128, 128), F32),
        ],
        scratch_shapes=[
            pltpu.VMEM((tokens + 2 * RIM, width), BF16),
            pltpu.VMEM((tokens, width), BF16),
            pltpu.VMEM((tokens, width), BF16),
            pltpu.VMEM((chunks, N, Q), F32),
            pltpu.VMEM((tokens, N), BF16),
            pltpu.VMEM((tokens, N), BF16),
            pltpu.VMEM((tokens, 128), F32),
            pltpu.VMEM((chunks, heads, Q), F32),
            pltpu.VMEM((chunks, heads, Q), F32),
            pltpu.VMEM((8, tokens), F32),
            pltpu.VMEM((chunks, heads, 128), F32),
            pltpu.VMEM((chunks, heads, 128), F32),
            pltpu.VMEM((chunks, heads, 128), F32),
            pltpu.VMEM((chunks, heads, 128), F32),
            pltpu.VMEM((chunks, heads, N, P_SIZE), BF16),
            pltpu.VMEM((2, heads, N, P_SIZE), F32),
            pltpu.VMEM((tokens + 2 * RIM, 2 * N), BF16),
            pltpu.VMEM((4, wide), F32),
            pltpu.VMEM((heads, P_SIZE), F32),
            pltpu.VMEM((2 * chunks, 3 * Q // 2, RIM + Q // 2), BF16),
            pltpu.VMEM((Q, Q), F32),
            pltpu.VMEM((chunks, Q, Q), F32),
            pltpu.VMEM((chunks, Q, P_SIZE), F32),
            pltpu.VMEM((chunks, Q // 128, 128), F32),
            pltpu.VMEM((2, RIM, wide), BF16),
            pltpu.VMEM((2, RIM, wide), BF16),
            pltpu.VMEM((2, RIM, wide), BF16),
            pltpu.VMEM((heads, 2, MESSAGE, P_SIZE), BF16),
            pltpu.VMEM((n_seq, 2, MESSAGE, P_SIZE), BF16),
            pltpu.VMEM((n_seq, 2, N, P_SIZE), BF16),
            (pltpu.VMEM((heads // SETS, 2, N, P_SIZE), BF16),) * SETS,
            pltpu.VMEM((n_head, chunks, Q // 128, 128), F32),
            dma(chunks), dma(chunks), dma(chunks), dma(2), dma(2), dma(2),
            dma(heads), dma(n_seq), dma(n_seq), dma(heads), dma(n_head), dma(n_head),
        ],
        compiler_params=pltpu.CompilerParams(
            vmem_limit_bytes=VMEM_MAIN * MIB,
            **(dict(collective_id=0, has_side_effects=True) if comm else {}),
        ),
        name="main",
    )(inputs, gates, *small, positions)


def norm_kernel(gated_ref, scale_ref, gain_ref, out_ref):
    for k in range(scale_ref.shape[0]):
        scale = scale_ref[k]
        row = jnp.concatenate([scale[0:1], scale[1:2]], axis=1)
        col = jnp.transpose(jnp.broadcast_to(row, (128, Q)))
        at = slice(k * Q, (k + 1) * Q)
        for c in range(gated_ref.shape[1] // 128):
            c0, c1 = c * 128, (c + 1) * 128
            out_ref[at, c0:c1] = (gated_ref[at, c0:c1].astype(F32) * col * gain_ref[:, c0:c1]).astype(BF16)


def norm_call(gated, scale, gain):
    tokens, width = gated.shape
    block = 2 * Q
    rows = pl.BlockSpec((block, width), lambda i: (i, 0))
    return pl.pallas_call(
        norm_kernel,
        grid=(tokens // block,),
        in_specs=[
            rows, pl.BlockSpec((block // Q, Q // 128, 128), lambda i: (i, 0, 0)),
            pl.BlockSpec((1, width), lambda i: (0, 0)),
        ],
        out_specs=rows,
        out_shape=jax.ShapeDtypeStruct((tokens, width), BF16),
        compiler_params=pltpu.CompilerParams(vmem_limit_bytes=60 * MIB),
        name="norm",
    )(gated, scale, gain)


def on_device(
    inputs, gates, writes, reads, step_raw, step_bias, decay_rate, skip_gain,
    conv_inputs, conv_writes, conv_reads, norm_gain, positions, segments,
    comm=True, phases=5,
):
    tokens, width = inputs.shape
    half_rows = tokens // 2
    n_seq = lax.axis_size("seq") if comm else 16
    n_head = lax.axis_size("head") if comm else 8
    small = (
        writes, reads, step_raw, step_bias[None], decay_rate[None], skip_gain[None],
        conv_inputs, conv_writes, conv_reads, segments.reshape(-1, half_rows // 128, 128),
    )
    gated, scale = main_call(n_seq, n_head, comm, phases, inputs, gates, small, positions)
    return norm_call(gated, scale, norm_gain[None])


def solution(mesh):
    return jax.shard_map(
        on_device,
        mesh=mesh,
        in_specs=(
            P("seq", "head"), P("seq", "head"), P("seq", "head"), P("seq", "head"), P("head", "seq"),
            P("head"), P("head"), P("head"), P(None, "head"), P(None, "head"), P(None, "head"),
            P("head"), P("seq"), P(),
        ),
        out_specs=P("seq", "head"),
        check_vma=False,
    )
```

time: 111 us -> 91.1 us (0.82)
  Pallas kernels: 92.1 us -> 81.4 us
  between operations: 4.95 us -> 0.03 us
  other arithmetic: 2.44 us -> 0 us
  local copies, waits for them, and re-layouts: 11.2 us -> 9.21 us
    pallas_call x1, Pallas kernels: 87.5 us -> 73.4 us  [main_call(): pl.pallas_call(functools.partial(main_kernel, n_seq, n_head, comm, phases...]
    unnamed x12 -> x24, local copies, waits for them, and re-layouts: 4.2 us -> 9.21 us
    pallas_call x1, Pallas kernels: 4.54 us -> 7.95 us  [norm_call(): pl.pallas_call(norm_kernel, grid=(tokens // block,), in_specs=[rows, pl.B...]
    broadcast_in_dim x5 -> x0, local copies, waits for them, and re-layouts: 3.37 us -> none  [the longest x1 1.32 us: on_device(): step_bias[:, None]]
    mul x2 -> x0, other arithmetic: 2.04 us -> none  [the longest x1 1.38 us: on_device(): jnp.concatenate([conv_inputs, conv_writes, conv_reads], axis=1).astype(F32)]
    slice x3 -> x0, local copies, waits for them, and re-layouts: 1.41 us -> none  [the longest x1 1.22 us: on_device(): first_start, second_start = (positions[0], positions[half_rows])]
where the time goes in v3:
time: 91.1 us; the launch traced here: 90.6 us
  Pallas kernels  81.4 us (89%)
  local copies, waits for them, and re-layouts  9.21 us (10%)
    pallas_call x1, Pallas kernels, main_call(): pl.pallas_call(functools.partial(main_kernel, n_seq, n_head, comm, phases...  73.4 us
    unnamed x24, local copies, waits for them, and re-layouts  9.21 us
    pallas_call x1, Pallas kernels, norm_call(): pl.pallas_call(norm_kernel, grid=(tokens // block,), in_specs=[rows, pl.B...  7.95 us

profile of v3, /device:TPU:1, one launch (start us, length us, event | category | flops | bytes accessed | tf_op | source)
XLA Modules:
  0.0 90.6 jit_solution(10728393353979323262)
XLA Ops:
  0.0 0.0 copy-start
  0.0 1.0 %copy-done = bf16[2048,128]{1,0:T(8,128)(2,1)S(1)} copy-done((bf16[2048,128]{1,0:T(8,128)(2,1)S(1)}, bf16[2048,128]{1,0:T(8,128)(2,1)}, u32[]{:S(2)}) %copy-start) | copy-done | bytes 524312
  1.0 0.0 copy-start.1
  1.0 1.0 %copy-done.1 = bf16[2048,128]{1,0:T(8,128)(2,1)S(1)} copy-done((bf16[2048,128]{1,0:T(8,128)(2,1)S(1)}, bf16[2048,128]{1,0:T(8,128)(2,1)}, u32[]{:S(2)}) %copy-start.1) | copy-done | bytes 524312
  2.1 0.0 copy-start.2
  2.1 0.9 copy-done.2
  3.0 0.0 copy-start.3
  3.0 0.9 copy-done.3
  3.9 0.0 copy-start.4
  3.9 0.7 copy-done.4
  4.6 0.0 copy-start.6
  4.6 0.7 copy-done.6
  5.3 0.0 copy-start.7
  5.3 0.7 copy-done.7
  6.0 0.0 copy-start.8
  6.0 0.7 copy-done.8
  6.7 0.0 copy-start.9
  6.7 0.7 copy-done.9
  7.3 0.0 copy-start.10
  7.3 0.7 copy-done.10
  8.0 0.0 copy-start.11
  8.0 0.7 copy-done.11
  8.6 73.4 %main.1 = (bf16[2048,2048]{1,0:T(8,128)(2,1)}, f32[8,2,128]{2,1,0:T(2,128)S(1)}) custom-call(bf16[2048,2048]{1,0:T(8,128)(2,1)} %x_hbm.1, bf16[2048,2048]{1,0:T(8,128)(2,1)} %gate_hbm.1, bf16[2048,128]{1,0:T(8,128)(2,1)S(1)} %copy-done, bf16[2048,128]{1,0:T(8,128)(2,1)S(1)} %copy-done.1, f32[16,2048]{1,0:T(8,128)S(1)} %copy-done.2, f32[1,16]{1,0:T(1,128)S(1)} %bitcast.6, ...), custom_call_target="tpu_custom_call" | custom-call | tf_op jit(solution)/shard_map/main/pallas_call | solution.py:466
  82.1 0.0 copy-start.5
  82.1 0.6 copy-done.5
  82.7 8.0 %norm.1 = bf16[2048,2048]{1,0:T(8,128)(2,1)} custom-call(bf16[2048,2048]{1,0:T(8,128)(2,1)} %get-tuple-element.7.gated_ref, f32[8,2,128]{2,1,0:T(2,128)} %copy-done.5, f32[1,2048]{1,0:T(1,128)} %bitcast.9), custom_call_target="tpu_custom_call" | custom-call | tf_op jit(solution)/shard_map/norm/pallas_call | solution.py:533
Async XLA Ops:
  0.0 1.0 %copy-start = (bf16[2048,128]{1,0:T(8,128)(2,1)S(1)}, bf16[2048,128]{1,0:T(8,128)(2,1)}, u32[]{:S(2)}) copy-start(bf16[2048,128]{1,0:T(8,128)(2,1)} %write_ref.1) | copy-start | bytes 1572868
  1.0 1.0 %copy-start.1 = (bf16[2048,128]{1,0:T(8,128)(2,1)S(1)}, bf16[2048,128]{1,0:T(8,128)(2,1)}, u32[]{:S(2)}) copy-start(bf16[2048,128]{1,0:T(8,128)(2,1)} %read_ref.1) | copy-start | bytes 1572868
  2.1 0.9 copy-start.2
  3.0 0.9 copy-start.3
  3.9 0.7 copy-start.4
  4.6 0.7 copy-start.6
  5.3 0.7 copy-start.7
  6.0 0.7 copy-start.8
  6.7 0.7 copy-start.9
  7.3 0.7 copy-start.10
  8.0 0.7 copy-start.11
  82.1 0.6 copy-start.5

commit v4 on v3

--- a/solution.py
+++ b/solution.py
@@ -12,9 +12,10 @@
 N = 128
 G = 8
 Q = 256
-SETS = 2
-SCAN_AT = (4, 12)
-VMEM_MAIN = 52
+SETS = 4
+VMEM_MAIN = 60
+SCAN_AFTER_SENDING = ((), (), (0,), ())
+SCAN_AFTER_INNER = {0: (1,), 1: (2,), 4: (3,)}
 EPSILON = 1e-05
 LOG2E = 1.4426950408889634
 MESH = pl.DeviceIdType.MESH
@@ -55,8 +56,8 @@
     x_hbm, gate_hbm, write_ref, read_ref, step_ref, bias_ref, rate_ref, skip_ref, ci_ref, cw_ref, cr_ref,
     seg_ref, pos_ref,
     out_hbm, scale_ref,
-    raw, feats, gate, wct, r_enter, r_half, cols, frow, trow, segs, decay, half_decay, loc_scale, half_scale,
-    sloc, state, raw_group, taps, skips, shifts, upper, scores, squares, sq, rim_own, rim_mine, rim_in,
+    raw, feats, gate, wct, wc, r_enter, r_half, cols, frow, trow, segs, decay, half_decay, loc_scale, half_scale,
+    sloc, state, raw_group, taps, skips, shifts, upper, scores, sq, rim_own, rim_mine, rim_in,
     msg, recv, back, entering, sums,
     x_sem, g_sem, o_sem, t_sem, h_send, h_recv, s1, r1, s2, r2, s3, r3,
 ):
@@ -238,28 +239,32 @@
             out.append(silu_of_half(total))
         return jnp.concatenate(out, axis=0)
 
-    def group_part(c, _):
+    def write_part(c, _):
         info = cols[rows_of(c)]
         for b in (0, 1):
             for k in (1, 2, 3):
                 same = spread_out(info[b * side : (b + 1) * side], INFO + k, RIM + side)
                 hit = jnp.where(from_row == to_row + (RIM - k), same, 0.0)
                 shifts[2 * c + b, (k - 1) * side : k * side] = hit.astype(BF16)
-        both = conv(raw_group, c, slice(0, 2 * N), slice(width, width + 2 * N))
-        w, r = both[:, :N], both[:, N:]
-        wct[c] = jnp.transpose(w.astype(BF16).astype(F32))
-        w, r = w.astype(BF16), r.astype(BF16)
+        w = conv(raw_group, c, slice(0, N), slice(width, width + N)).astype(BF16)
+        wc[rows_of(c)] = w
+        wct[c] = jnp.transpose(w.astype(F32))
+        return 0
+
+    if phases >= 2:
+        lax.fori_loop(0, chunks, write_part, 0, unroll=2)
+
+    def read_part(c, _):
+        info = cols[rows_of(c)]
+        r = conv(raw_group, c, slice(N, 2 * N), slice(width + N, width + 2 * N)).astype(BF16)
         wide = r.astype(F32)
         r_enter[rows_of(c)] = (wide * spread_out(info, INFO + 4)).astype(BF16)
         r_half[rows_of(c)] = (wide * spread_out(info, INFO + 5)).astype(BF16)
-        full = lax.dot_general(r, w, (((1,), (1,)), ((), ())), preferred_element_type=F32)
+        full = lax.dot_general(r, wc[rows_of(c)], (((1,), (1,)), ((), ())), preferred_element_type=F32)
         seg_row = segs[0:1, lanes_of(c * Q, Q)]
         keep = (info[:, INFO : INFO + 1] == seg_row) & (col <= row)
         scores[c] = jnp.where(keep, full, 0.0)
         return 0
-
-    if phases >= 2:
-        lax.fori_loop(0, chunks, group_part, 0)
 
     def conv_part(g, c, _):
         if g == 0:
@@ -340,19 +345,19 @@
 
     if phases >= 3:
         for g in range(SETS):
-            lax.fori_loop(0, chunks, functools.partial(conv_part, g), 0)
-            lax.fori_loop(0, chunks, functools.partial(state_part, g), 0)
+            lax.fori_loop(0, chunks, functools.partial(conv_part, g), 0, unroll=2)
+            lax.fori_loop(0, chunks, functools.partial(state_part, g), 0, unroll=4)
             send_states(g)
-
-    def inner_part(g, c, _):
+            for scanned in SCAN_AFTER_SENDING[g]:
+                scan_states(scanned)
+
+    def inner_part(c, _):
         info = cols[rows_of(c)]
-        if g == 0:
-            gate_copy(c).wait()
+        gate_copy(c).wait()
 
         masked = scores[c]
         r = r_enter[rows_of(c)]
-        for j in range(per_set):
-            h = g * per_set + j
+        for h in range(heads):
             one = slice(h * P_SIZE, (h + 1) * P_SIZE)
             feat = feats[rows_of(c), one]
             fac = frow[c, h : h + 1, :]
@@ -373,55 +378,45 @@
             raw[rows_of(c), one] = y.astype(BF16)
         return 0
 
-    def inner_steps(start, stop):
-        for g in range(SETS):
-            begin, end = max(start - g * chunks, 0), min(stop - g * chunks, chunks)
-            if begin < end:
-                lax.fori_loop(begin, end, functools.partial(inner_part, g), 0)
-
     if phases >= 4:
+        lax.fori_loop(0, chunks, read_part, 0, unroll=2)
         done = 0
-        for g, until in enumerate(SCAN_AT):
-            inner_steps(done, until)
-            scan_states(g)
+        for until, scanned in [*SCAN_AFTER_INNER.items(), (chunks, ())]:
+            lax.fori_loop(done, until, inner_part, 0)
             done = until
-        inner_steps(done, SETS * chunks)
-
-    def finish_part(g, c, _):
+            for g in scanned:
+                scan_states(g)
+
+    def finish_part(c, _):
         r = r_half[rows_of(c)]
         which = jnp.where(c >= per_half, 1 - flip, flip)
-        total = jnp.zeros((Q, P_SIZE), F32) if g == 0 else squares[c]
-        for pair in range(per_set // 2):
+        total = jnp.zeros((Q, P_SIZE), F32)
+        for pair in range(heads // 2):
             states = []
-            for j in (0, 1):
-                h = g * per_set + 2 * pair + j
-                states.append((entering[g][2 * pair + j, which].astype(F32) * half_scale[c, h : h + 1, :]).astype(BF16))
+            for h in (2 * pair, 2 * pair + 1):
+                state_in = entering[h // per_set][h % per_set, which].astype(F32)
+                states.append((state_in * half_scale[c, h : h + 1, :]).astype(BF16))
             inter = jnp.dot(r, jnp.concatenate(states, axis=1), preferred_element_type=F32)
             for j in (0, 1):
-                start = g * set_width + (2 * pair + j) * P_SIZE
+                start = (2 * pair + j) * P_SIZE
                 one = slice(start, start + P_SIZE)
                 gated = raw[rows_of(c), one].astype(F32)
                 gated = gated + inter[:, j * P_SIZE : (j + 1) * P_SIZE] * gate[rows_of(c), one].astype(F32)
                 total = total + gated * gated
                 feats[rows_of(c), one] = gated.astype(BF16)
-        if g < SETS - 1:
-            squares[c] = total
-        else:
-            out_copy(c).start()
-            sums_here = jnp.sum(jnp.transpose(total), axis=0, keepdims=True)
-            sq[c] = jnp.concatenate([sums_here[:, :128], sums_here[:, 128:]], axis=0)
-
+        out_copy(c).start()
+        sums_here = jnp.sum(jnp.transpose(total), axis=0, keepdims=True)
+        sq[c] = jnp.concatenate([sums_here[:, :128], sums_here[:, 128:]], axis=0)
         return 0
 
-    for g in range(SETS):
-        if comm:
-            for h in range(g * per_set, (g + 1) * per_set):
-                @pl.when(me != device_of[h])
-                def _():
-                    enter_copy(g, h, device_of[h]).wait_recv()
-
-        if phases >= 5:
-            lax.fori_loop(0, chunks, functools.partial(finish_part, g), 0)
+    if comm:
+        for h in range(heads):
+            @pl.when(me != device_of[h])
+            def _():
+                enter_copy(h // per_set, h, device_of[h]).wait_recv()
+
+    if phases >= 5:
+        lax.fori_loop(0, chunks, finish_part, 0)
 
     total = sq[...]
     if comm:
@@ -478,6 +473,7 @@
             pltpu.VMEM((chunks, N, Q), F32),
             pltpu.VMEM((tokens, N), BF16),
             pltpu.VMEM((tokens, N), BF16),
+            pltpu.VMEM((tokens, N), BF16),
             pltpu.VMEM((tokens, 128), F32),
             pltpu.VMEM((chunks, heads, Q), F32),
             pltpu.VMEM((chunks, heads, Q), F32),
@@ -494,7 +490,6 @@
             pltpu.VMEM((2 * chunks, 3 * Q // 2, RIM + Q // 2), BF16),
             pltpu.VMEM((Q, Q), F32),
             pltpu.VMEM((chunks, Q, Q), F32),
-            pltpu.VMEM((chunks, Q, P_SIZE), F32),
             pltpu.VMEM((chunks, Q // 128, 128), F32),
             pltpu.VMEM((2, RIM, wide), BF16),
             pltpu.VMEM((2, RIM, wide), BF16),
@@ -515,30 +510,46 @@
     )(inputs, gates, *small, positions)
 
 
-def norm_kernel(gated_ref, scale_ref, gain_ref, out_ref):
-    for k in range(scale_ref.shape[0]):
-        scale = scale_ref[k]
-        row = jnp.concatenate([scale[0:1], scale[1:2]], axis=1)
-        col = jnp.transpose(jnp.broadcast_to(row, (128, Q)))
-        at = slice(k * Q, (k + 1) * Q)
-        for c in range(gated_ref.shape[1] // 128):
-            c0, c1 = c * 128, (c + 1) * 128
-            out_ref[at, c0:c1] = (gated_ref[at, c0:c1].astype(F32) * col * gain_ref[:, c0:c1]).astype(BF16)
+def norm_kernel(gated_hbm, scale_ref, gain_ref, out_hbm, rows, in_sem, out_sem):
+    chunks = scale_ref.shape[0]
+
+    def part(c):
+        return pl.ds(c * Q, Q)
+
+    def in_copy(c):
+        return pltpu.make_async_copy(gated_hbm.at[part(c)], rows.at[part(c)], in_sem.at[c])
+
+    def out_copy(c):
+        return pltpu.make_async_copy(rows.at[part(c)], out_hbm.at[part(c)], out_sem.at[c])
+
+    for c in range(chunks):
+        in_copy(c).start()
+    for c in range(chunks):
+        scale = scale_ref[c]
+        line = jnp.concatenate([scale[0:1], scale[1:2]], axis=1)
+        col = jnp.transpose(jnp.broadcast_to(line, (128, Q)))
+        in_copy(c).wait()
+        for k in range(rows.shape[1] // 128):
+            at = slice(k * 128, (k + 1) * 128)
+            rows[part(c), at] = (rows[part(c), at].astype(F32) * col * gain_ref[:, at]).astype(BF16)
+        out_copy(c).start()
+    for c in range(chunks):
+        out_copy(c).wait()
 
 
 def norm_call(gated, scale, gain):
     tokens, width = gated.shape
-    block = 2 * Q
-    rows = pl.BlockSpec((block, width), lambda i: (i, 0))
+    vmem = pl.BlockSpec(memory_space=pltpu.VMEM)
+    hbm = pl.BlockSpec(memory_space=pl.ANY)
     return pl.pallas_call(
         norm_kernel,
-        grid=(tokens // block,),
-        in_specs=[
-            rows, pl.BlockSpec((block // Q, Q // 128, 128), lambda i: (i, 0, 0)),
-            pl.BlockSpec((1, width), lambda i: (0, 0)),
+        in_specs=[hbm, vmem, vmem],
+        out_specs=hbm,
+        out_shape=jax.ShapeDtypeStruct((tokens, width), BF16),
+        scratch_shapes=[
+            pltpu.VMEM((tokens, width), BF16),
+            pltpu.SemaphoreType.DMA((tokens // Q,)), pltpu.SemaphoreType.DMA((tokens // Q,)),
         ],
-        out_specs=rows,
-        out_shape=jax.ShapeDtypeStruct((tokens, width), BF16),
         compiler_params=pltpu.CompilerParams(vmem_limit_bytes=60 * MIB),
         name="norm",
     )(gated, scale, gain)

time: 91.1 us -> 85.8 us (0.942)
  local copies, waits for them, and re-layouts: 9.21 us -> 0 us
  Pallas kernels: 81.4 us -> 85.4 us
    unnamed x24 -> x0, local copies, waits for them, and re-layouts: 9.21 us -> none
    pallas_call x1, Pallas kernels: 73.4 us -> 78 us  [main_call(): pl.pallas_call(functools.partial(main_kernel, n_seq, n_head, comm, phases...]
where the time goes in v4:
time: 85.8 us; the launch traced here: 85.6 us
  Pallas kernels  85.4 us (100%)
    pallas_call x1, Pallas kernels, main_call(): pl.pallas_call(functools.partial(main_kernel, n_seq, n_head, comm, phases...  78 us
    pallas_call x1, Pallas kernels, norm_call(): pl.pallas_call(norm_kernel, in_specs=[hbm, vmem, vmem], out_specs=hbm, ou...  7.44 us

profile of v4, /device:TPU:1, one launch (start us, length us, event | category | flops | bytes accessed | tf_op | source)
XLA Modules:
  0.0 85.6 jit_solution(14904858263729006438)
XLA Ops:
  0.0 78.0 %main.1 = (bf16[2048,2048]{1,0:T(8,128)(2,1)}, f32[8,2,128]{2,1,0:T(2,128)}) custom-call(bf16[2048,2048]{1,0:T(8,128)(2,1)} %x_hbm.1, bf16[2048,2048]{1,0:T(8,128)(2,1)} %gate_hbm.1, bf16[2048,128]{1,0:T(8,128)(2,1)} %write_ref.1, bf16[2048,128]{1,0:T(8,128)(2,1)} %read_ref.1, f32[16,2048]{1,0:T(8,128)} %step_ref.1, f32[1,16]{1,0:T(1,128)} %bitcast.7, ...), custom_call_target="tpu_custom_call" | custom-call | tf_op jit(solution)/shard_map/main/pallas_call | solution.py:461
  78.0 7.4 %norm.1 = bf16[2048,2048]{1,0:T(8,128)(2,1)} custom-call(bf16[2048,2048]{1,0:T(8,128)(2,1)} %get-tuple-element.7.gated_hbm, f32[8,2,128]{2,1,0:T(2,128)} %get-tuple-element.8.scale_ref, f32[1,2048]{1,0:T(1,128)} %bitcast.6), custom_call_target="tpu_custom_call" | custom-call | tf_op jit(solution)/shard_map/norm/pallas_call | solution.py:544

commit v5 on v4

--- a/solution.py
+++ b/solution.py
@@ -14,15 +14,14 @@
 Q = 256
 SETS = 4
 VMEM_MAIN = 60
-SCAN_AFTER_SENDING = ((), (), (0,), ())
-SCAN_AFTER_INNER = {0: (1,), 1: (2,), 4: (3,)}
+SCAN_AFTER_SENDING = ((), (), (0,), (1,))
+SCAN_AFTER_INNER = {1: (2,), 4: (3,)}
 EPSILON = 1e-05
 LOG2E = 1.4426950408889634
 MESH = pl.DeviceIdType.MESH
 MIB = 2**20
 F32 = jnp.float32
 BF16 = jnp.bfloat16
-MESSAGE = N + 16
 RIM = 16
 
 
@@ -32,23 +31,6 @@
 
 def spread_out(cols, lane, width=P_SIZE):
     return jnp.broadcast_to(cols[:, lane : lane + 1], (cols.shape[0], width))
-
-
-def scan_device(h, n):
-    side = 4 if n == 16 else 1
-    per_set = n // SETS
-    g, j = h // per_set, h % per_set
-    per_row = per_set // side
-    y = j // per_row
-    return y * (n // side) + (j % per_row) * SETS + (g - y) % SETS
-
-
-def scan_head(me, n):
-    side = 4 if n == 16 else 1
-    per_row = n // SETS // side
-    y, z = me // (n // side), lax.rem(me, n // side)
-    g = lax.rem(y + z, SETS)
-    return g, g * (n // SETS) + y * per_row + z // SETS
 
 
 def main_kernel(
@@ -58,7 +40,7 @@
     out_hbm, scale_ref,
     raw, feats, gate, wct, wc, r_enter, r_half, cols, frow, trow, segs, decay, half_decay, loc_scale, half_scale,
     sloc, state, raw_group, taps, skips, shifts, upper, scores, sq, rim_own, rim_mine, rim_in,
-    msg, recv, back, entering, sums,
+    msg, recv, scanned, back, entering, whole, sums,
     x_sem, g_sem, o_sem, t_sem, h_send, h_recv, s1, r1, s2, r2, s3, r3,
 ):
     tokens, width = feats.shape
@@ -71,8 +53,9 @@
     side = Q // 2
     me = lax.axis_index("seq") if comm else 0
     my_head = lax.axis_index("head") if comm else 0
-    my_set, my_scan = scan_head(me, n_seq)
-    device_of = [scan_device(h, n_seq) for h in range(heads)]
+    slice_rows = N // n_seq
+    block = 2 * slice_rows
+    states_rows = per_set * block
     CUM, INFO = 0, heads
     first, second = pos_ref[0], pos_ref[half_rows]
     flip = jnp.where(first > second, 1, 0)
@@ -287,69 +270,83 @@
             state[half, h] = old * decay[c, one, :] + add
         return 0
 
-    def state_copy(h):
+    def state_copy(g, k, src):
+        to = lax.rem(me + k, n_seq)
         return pltpu.make_async_remote_copy(
-            src_ref=msg.at[h], dst_ref=recv.at[me], send_sem=s1.at[h], recv_sem=r1.at[me],
-            device_id={"seq": device_of[h]}, device_id_type=MESH,
+            src_ref=msg.at[g, to], dst_ref=recv.at[g, src], send_sem=s1.at[g * n_seq + k],
+            recv_sem=r1.at[g * n_seq + k], device_id={"seq": to}, device_id_type=MESH,
         )
 
-    def state_arrival(src):
+    def enter_copy(g, k, src):
+        to = lax.rem(me + k, n_seq)
         return pltpu.make_async_remote_copy(
-            src_ref=msg.at[0], dst_ref=recv.at[src], send_sem=s1.at[0], recv_sem=r1.at[src],
-            device_id={"seq": src}, device_id_type=MESH,
+            src_ref=back.at[g, to], dst_ref=entering.at[g, src], send_sem=s2.at[g * n_seq + k],
+            recv_sem=r2.at[g * n_seq + k], device_id={"seq": to}, device_id_type=MESH,
         )
 
-    def enter_copy(g, h, to):
-        return pltpu.make_async_remote_copy(
-            src_ref=back.at[to], dst_ref=entering[g].at[h - g * per_set], send_sem=s2.at[to], recv_sem=r2.at[h],
-            device_id={"seq": to}, device_id_type=MESH,
-        )
+    def behind(k):
+        return lax.rem(me + n_seq - k, n_seq)
 
     def send_states(g):
-        for h in range(g * per_set, (g + 1) * per_set):
-            for k, half in ((0, flip), (1, 1 - flip)):
-                msg[h, k, :N] = state[half, h].astype(BF16)
-                whole = jnp.broadcast_to(half_decay[(half + 1) * per_half - 1, h : h + 1], (8, 128))
-                high = whole.astype(BF16).astype(F32)
-                msg[h, k, N:] = jnp.concatenate([high, whole - high], axis=0).astype(BF16)
-            if comm:
-                to = device_of[h]
-
-                @pl.when(me != to)
-                def _():
-                    state_copy(h).start()
-
-                @pl.when(me == to)
-                def _():
-                    recv[me] = msg[h]
+        decays = []
+        for j in range(per_set):
+            h = g * per_set + j
+            both = []
+            for half in (flip, 1 - flip):
+                both.append(state[half, h].reshape(n_seq, slice_rows, P_SIZE))
+                kept = half_decay[(half + 1) * per_half - 1, h : h + 1]
+                high = kept.astype(BF16).astype(F32)
+                decays += [high, kept - high]
+            msg[g, :, j * block : (j + 1) * block] = jnp.concatenate(both, axis=1).astype(BF16)
+        lines = jnp.concatenate(decays, axis=0)
+        msg[g, :, states_rows:] = jnp.broadcast_to(lines[None], (n_seq, *lines.shape)).astype(BF16)
+        if comm:
+            for k in range(1, n_seq):
+                state_copy(g, k, me).start()
+            recv[g, me] = msg[g, me]
 
     def scan_states(g):
         if not comm:
             return
-
-        @pl.when(my_set == g)
-        def _():
-            for k in range(1, n_seq):
-                state_arrival(lax.rem(me + k, n_seq)).wait_recv()
-
-            def advance(total, src, half):
-                back[src, half] = total.astype(BF16)
-                keep = recv[src, half, N : N + 1].astype(F32) + recv[src, half, N + 8 : N + 9].astype(F32)
-                return total * keep + recv[src, half, :N].astype(F32)
-
-            total = lax.fori_loop(0, n_seq, lambda k, t: advance(t, k, 0), jnp.zeros((N, P_SIZE), F32))
-            lax.fori_loop(0, n_seq, lambda k, t: advance(t, n_seq - 1 - k, 1), total)
-            for k in range(1, n_seq):
-                enter_copy(g, my_scan, lax.rem(me + k, n_seq)).start()
-            entering[g][my_scan - g * per_set] = back[me]
+        for k in range(1, n_seq):
+            state_copy(g, k, behind(k)).wait_recv()
+
+        def advance(totals, src, half):
+            got = recv[g, src].astype(F32)
+            new = []
+            for j, total in enumerate(totals):
+                at = j * block + half * slice_rows
+                scanned[src, at : at + slice_rows] = total
+                line = states_rows + 4 * j + 2 * half
+                keep = got[line : line + 1] + got[line + 1 : line + 2]
+                new.append(total * keep + got[at : at + slice_rows])
+            return tuple(new)
+
+        totals = tuple(jnp.zeros((slice_rows, P_SIZE), F32) for _ in range(per_set))
+        totals = lax.fori_loop(0, n_seq, lambda k, t: advance(t, k, 0), totals, unroll=4)
+        lax.fori_loop(0, n_seq, lambda k, t: advance(t, n_seq - 1 - k, 1), totals, unroll=4)
+        back[g] = scanned[...].astype(BF16)
+        for k in range(1, n_seq):
+            enter_copy(g, k, me).start()
+        entering[g, me] = back[g, me]
+
+    def assemble(g):
+        for j in range(per_set):
+            h = g * per_set + j
+            both = entering[g, :, j * block : (j + 1) * block].astype(F32)
+            low = both[:, :slice_rows].reshape(N, P_SIZE)
+            high = both[:, slice_rows:].reshape(N, P_SIZE)
+            swap = jnp.full(low.shape, flip) > 0
+            whole[0, h] = jnp.where(swap, high, low).astype(BF16)
+            whole[1, h] = jnp.where(swap, low, high).astype(BF16)
 
     if phases >= 3:
         for g in range(SETS):
             lax.fori_loop(0, chunks, functools.partial(conv_part, g), 0, unroll=2)
             lax.fori_loop(0, chunks, functools.partial(state_part, g), 0, unroll=4)
             send_states(g)
-            for scanned in SCAN_AFTER_SENDING[g]:
-                scan_states(scanned)
+            for ready in SCAN_AFTER_SENDING[g]:
+                scan_states(ready)
 
     def inner_part(c, _):
         info = cols[rows_of(c)]
@@ -381,20 +378,20 @@
     if phases >= 4:
         lax.fori_loop(0, chunks, read_part, 0, unroll=2)
         done = 0
-        for until, scanned in [*SCAN_AFTER_INNER.items(), (chunks, ())]:
+        for until, ready in [*SCAN_AFTER_INNER.items(), (chunks, ())]:
             lax.fori_loop(done, until, inner_part, 0)
             done = until
-            for g in scanned:
+            for g in ready:
                 scan_states(g)
 
     def finish_part(c, _):
         r = r_half[rows_of(c)]
-        which = jnp.where(c >= per_half, 1 - flip, flip)
+        half = c // per_half
         total = jnp.zeros((Q, P_SIZE), F32)
         for pair in range(heads // 2):
             states = []
             for h in (2 * pair, 2 * pair + 1):
-                state_in = entering[h // per_set][h % per_set, which].astype(F32)
+                state_in = whole[half, h].astype(F32)
                 states.append((state_in * half_scale[c, h : h + 1, :]).astype(BF16))
             inter = jnp.dot(r, jnp.concatenate(states, axis=1), preferred_element_type=F32)
             for j in (0, 1):
@@ -409,11 +406,11 @@
         sq[c] = jnp.concatenate([sums_here[:, :128], sums_here[:, 128:]], axis=0)
         return 0
 
-    if comm:
-        for h in range(heads):
-            @pl.when(me != device_of[h])
-            def _():
-                enter_copy(h // per_set, h, device_of[h]).wait_recv()
+    for g in range(SETS):
+        if comm:
+            for k in range(1, n_seq):
+                enter_copy(g, k, behind(k)).wait_recv()
+        assemble(g)
 
     if phases >= 5:
         lax.fori_loop(0, chunks, finish_part, 0)
@@ -429,12 +426,10 @@
                 )
             )
             copies[-1].start()
-        for h in range(heads):
-            @pl.when(me != device_of[h])
-            def _():
-                state_copy(h).wait_send()
-        for k in range(1, n_seq):
-            enter_copy(0, 0, lax.rem(me + k, n_seq)).wait_send()
+        for g in range(SETS):
+            for k in range(1, n_seq):
+                state_copy(g, k, me).wait_send()
+                enter_copy(g, k, me).wait_send()
         for k in range(1, n_head):
             copies[k - 1].wait()
             total = total + sums[k]
@@ -455,6 +450,7 @@
     heads = width // P_SIZE
     chunks = tokens // Q
     wide = width + 2 * N
+    rows = heads // SETS * 2 * N // n_seq
     vmem = pl.BlockSpec(memory_space=pltpu.VMEM)
     hbm = pl.BlockSpec(memory_space=pl.ANY)
     dma = lambda n: pltpu.SemaphoreType.DMA((n,))
@@ -494,13 +490,15 @@
             pltpu.VMEM((2, RIM, wide), BF16),
             pltpu.VMEM((2, RIM, wide), BF16),
             pltpu.VMEM((2, RIM, wide), BF16),
-            pltpu.VMEM((heads, 2, MESSAGE, P_SIZE), BF16),
-            pltpu.VMEM((n_seq, 2, MESSAGE, P_SIZE), BF16),
-            pltpu.VMEM((n_seq, 2, N, P_SIZE), BF16),
-            (pltpu.VMEM((heads // SETS, 2, N, P_SIZE), BF16),) * SETS,
+            pltpu.VMEM((SETS, n_seq, rows + 16, P_SIZE), BF16),
+            pltpu.VMEM((SETS, n_seq, rows + 16, P_SIZE), BF16),
+            pltpu.VMEM((n_seq, rows, P_SIZE), F32),
+            pltpu.VMEM((SETS, n_seq, rows, P_SIZE), BF16),
+            pltpu.VMEM((SETS, n_seq, rows, P_SIZE), BF16),
+            pltpu.VMEM((2, heads, N, P_SIZE), BF16),
             pltpu.VMEM((n_head, chunks, Q // 128, 128), F32),
             dma(chunks), dma(chunks), dma(chunks), dma(2), dma(2), dma(2),
-            dma(heads), dma(n_seq), dma(n_seq), dma(heads), dma(n_head), dma(n_head),
+            *[dma(SETS * n_seq)] * 4, dma(n_head), dma(n_head),
         ],
         compiler_params=pltpu.CompilerParams(
             vmem_limit_bytes=VMEM_MAIN * MIB,

time: 85.8 us -> 73.5 us (0.86)
  Pallas kernels: 85.4 us -> 73.1 us
    pallas_call x1, Pallas kernels: 78 us -> 65.7 us  [main_call(): pl.pallas_call(functools.partial(main_kernel, n_seq, n_head, comm, phases...]
where the time goes in v5:
time: 73.5 us; the launch traced here: 73.3 us
  Pallas kernels  73.1 us (99%)
    pallas_call x1, Pallas kernels, main_call(): pl.pallas_call(functools.partial(main_kernel, n_seq, n_head, comm, phases...  65.7 us
    pallas_call x1, Pallas kernels, norm_call(): pl.pallas_call(norm_kernel, in_specs=[hbm, vmem, vmem], out_specs=hbm, ou...  7.44 us

profile of v5, /device:TPU:1, one launch (start us, length us, event | category | flops | bytes accessed | tf_op | source)
XLA Modules:
  0.0 73.3 jit_solution(6580701169532409588)
XLA Ops:
  0.0 65.7 %main.1 = (bf16[2048,2048]{1,0:T(8,128)(2,1)}, f32[8,2,128]{2,1,0:T(2,128)}) custom-call(bf16[2048,2048]{1,0:T(8,128)(2,1)} %x_hbm.1, bf16[2048,2048]{1,0:T(8,128)(2,1)} %gate_hbm.1, bf16[2048,128]{1,0:T(8,128)(2,1)} %write_ref.1, bf16[2048,128]{1,0:T(8,128)(2,1)} %read_ref.1, f32[16,2048]{1,0:T(8,128)} %step_ref.1, f32[1,16]{1,0:T(1,128)} %bitcast.7, ...), custom_call_target="tpu_custom_call" | custom-call | tf_op jit(solution)/shard_map/main/pallas_call | solution.py:457
  65.7 7.4 %norm.1 = bf16[2048,2048]{1,0:T(8,128)(2,1)} custom-call(bf16[2048,2048]{1,0:T(8,128)(2,1)} %get-tuple-element.7.gated_hbm, f32[8,2,128]{2,1,0:T(2,128)} %get-tuple-element.8.scale_ref, f32[1,2048]{1,0:T(1,128)} %bitcast.6), custom_call_target="tpu_custom_call" | custom-call | tf_op jit(solution)/shard_map/norm/pallas_call | solution.py:542

commit v6 on v5

--- a/solution.py
+++ b/solution.py
@@ -270,22 +270,33 @@
             state[half, h] = old * decay[c, one, :] + add
         return 0
 
-    def state_copy(g, k, src):
+    def state_copy(g, k):
         to = lax.rem(me + k, n_seq)
         return pltpu.make_async_remote_copy(
-            src_ref=msg.at[g, to], dst_ref=recv.at[g, src], send_sem=s1.at[g * n_seq + k],
-            recv_sem=r1.at[g * n_seq + k], device_id={"seq": to}, device_id_type=MESH,
+            src_ref=msg.at[g, to], dst_ref=recv.at[g, me], send_sem=s1.at[g], recv_sem=r1.at[g],
+            device_id={"seq": to}, device_id_type=MESH,
         )
 
-    def enter_copy(g, k, src):
+    def all_states(g):
+        others = pl.ds(0, n_seq - 1)
+        return pltpu.make_async_remote_copy(
+            src_ref=msg.at[g, others], dst_ref=recv.at[g, others], send_sem=s1.at[g],
+            recv_sem=r1.at[g], device_id={"seq": lax.rem(me + 1, n_seq)}, device_id_type=MESH,
+        )
+
+    def all_entering(g):
+        others = pl.ds(0, n_seq - 1)
+        return pltpu.make_async_remote_copy(
+            src_ref=back.at[g, others], dst_ref=entering.at[g, others], send_sem=s2.at[g],
+            recv_sem=r2.at[g], device_id={"seq": lax.rem(me + 1, n_seq)}, device_id_type=MESH,
+        )
+
+    def enter_copy(g, k):
         to = lax.rem(me + k, n_seq)
         return pltpu.make_async_remote_copy(
-            src_ref=back.at[g, to], dst_ref=entering.at[g, src], send_sem=s2.at[g * n_seq + k],
-            recv_sem=r2.at[g * n_seq + k], device_id={"seq": to}, device_id_type=MESH,
+            src_ref=back.at[g, to], dst_ref=entering.at[g, me], send_sem=s2.at[g], recv_sem=r2.at[g],
+            device_id={"seq": to}, device_id_type=MESH,
         )
-
-    def behind(k):
-        return lax.rem(me + n_seq - k, n_seq)
 
     def send_states(g):
         decays = []
@@ -302,14 +313,13 @@
         msg[g, :, states_rows:] = jnp.broadcast_to(lines[None], (n_seq, *lines.shape)).astype(BF16)
         if comm:
             for k in range(1, n_seq):
-                state_copy(g, k, me).start()
+                state_copy(g, k).start()
             recv[g, me] = msg[g, me]
 
     def scan_states(g):
         if not comm:
             return
-        for k in range(1, n_seq):
-            state_copy(g, k, behind(k)).wait_recv()
+        all_states(g).wait_recv()
 
         def advance(totals, src, half):
             got = recv[g, src].astype(F32)
@@ -327,7 +337,7 @@
         lax.fori_loop(0, n_seq, lambda k, t: advance(t, n_seq - 1 - k, 1), totals, unroll=4)
         back[g] = scanned[...].astype(BF16)
         for k in range(1, n_seq):
-            enter_copy(g, k, me).start()
+            enter_copy(g, k).start()
         entering[g, me] = back[g, me]
 
     def assemble(g):
@@ -408,8 +418,7 @@
 
     for g in range(SETS):
         if comm:
-            for k in range(1, n_seq):
-                enter_copy(g, k, behind(k)).wait_recv()
+            all_entering(g).wait_recv()
         assemble(g)
 
     if phases >= 5:
@@ -427,9 +436,8 @@
             )
             copies[-1].start()
         for g in range(SETS):
-            for k in range(1, n_seq):
-                state_copy(g, k, me).wait_send()
-                enter_copy(g, k, me).wait_send()
+            all_states(g).wait_send()
+            all_entering(g).wait_send()
         for k in range(1, n_head):
             copies[k - 1].wait()
             total = total + sums[k]
@@ -490,15 +498,15 @@
             pltpu.VMEM((2, RIM, wide), BF16),
             pltpu.VMEM((2, RIM, wide), BF16),
             pltpu.VMEM((2, RIM, wide), BF16),
-            pltpu.VMEM((SETS, n_seq, rows + 16, P_SIZE), BF16),
-            pltpu.VMEM((SETS, n_seq, rows + 16, P_SIZE), BF16),
+            pltpu.VMEM((SETS, n_seq, rows + 4 * heads // SETS, P_SIZE), BF16),
+            pltpu.VMEM((SETS, n_seq, rows + 4 * heads // SETS, P_SIZE), BF16),
             pltpu.VMEM((n_seq, rows, P_SIZE), F32),
             pltpu.VMEM((SETS, n_seq, rows, P_SIZE), BF16),
             pltpu.VMEM((SETS, n_seq, rows, P_SIZE), BF16),
             pltpu.VMEM((2, heads, N, P_SIZE), BF16),
             pltpu.VMEM((n_head, chunks, Q // 128, 128), F32),
             dma(chunks), dma(chunks), dma(chunks), dma(2), dma(2), dma(2),
-            *[dma(SETS * n_seq)] * 4, dma(n_head), dma(n_head),
+            *[dma(SETS)] * 4, dma(n_head), dma(n_head),
         ],
         compiler_params=pltpu.CompilerParams(
             vmem_limit_bytes=VMEM_MAIN * MIB,

time: 73.5 us -> 71.2 us (0.969)
  Pallas kernels: 73.1 us -> 70.8 us
    pallas_call x1, Pallas kernels: 65.7 us -> 63.4 us  [main_call(): pl.pallas_call(functools.partial(main_kernel, n_seq, n_head, comm, phases...]
where the time goes in v6:
time: 71.2 us; the launch traced here: 71 us
  Pallas kernels  70.8 us (99%)
    pallas_call x1, Pallas kernels, main_call(): pl.pallas_call(functools.partial(main_kernel, n_seq, n_head, comm, phases...  63.4 us
    pallas_call x1, Pallas kernels, norm_call(): pl.pallas_call(norm_kernel, in_specs=[hbm, vmem, vmem], out_specs=hbm, ou...  7.44 us

profile of v6, /device:TPU:1, one launch (start us, length us, event | category | flops | bytes accessed | tf_op | source)
XLA Modules:
  0.0 71.0 jit_solution(10156512919751051374)
XLA Ops:
  0.0 63.4 %main.1 = (bf16[2048,2048]{1,0:T(8,128)(2,1)}, f32[8,2,128]{2,1,0:T(2,128)}) custom-call(bf16[2048,2048]{1,0:T(8,128)(2,1)} %x_hbm.1, bf16[2048,2048]{1,0:T(8,128)(2,1)} %gate_hbm.1, bf16[2048,128]{1,0:T(8,128)(2,1)} %write_ref.1, bf16[2048,128]{1,0:T(8,128)(2,1)} %read_ref.1, f32[16,2048]{1,0:T(8,128)} %step_ref.1, f32[1,16]{1,0:T(1,128)} %bitcast.7, ...), custom_call_target="tpu_custom_call" | custom-call | tf_op jit(solution)/shard_map/main/pallas_call | solution.py:465
  63.4 7.4 %norm.1 = bf16[2048,2048]{1,0:T(8,128)(2,1)} custom-call(bf16[2048,2048]{1,0:T(8,128)(2,1)} %get-tuple-element.7.gated_hbm, f32[8,2,128]{2,1,0:T(2,128)} %get-tuple-element.8.scale_ref, f32[1,2048]{1,0:T(1,128)} %bitcast.6), custom_call_target="tpu_custom_call" | custom-call | tf_op jit(solution)/shard_map/norm/pallas_call | solution.py:550

commit v7 on v6

--- a/solution.py
+++ b/solution.py
@@ -235,7 +235,7 @@
         return 0
 
     if phases >= 2:
-        lax.fori_loop(0, chunks, write_part, 0, unroll=2)
+        lax.fori_loop(0, chunks, write_part, 0, unroll=4)
 
     def read_part(c, _):
         info = cols[rows_of(c)]
@@ -250,8 +250,6 @@
         return 0
 
     def conv_part(g, c, _):
-        if g == 0:
-            x_copy(c).wait()
         for pair in range(per_set // 2):
             start = g * set_width + pair * 2 * P_SIZE
             at = slice(start, start + 2 * P_SIZE)
@@ -351,16 +349,17 @@
             whole[1, h] = jnp.where(swap, low, high).astype(BF16)
 
     if phases >= 3:
+        for c in range(chunks):
+            x_copy(c).wait()
         for g in range(SETS):
-            lax.fori_loop(0, chunks, functools.partial(conv_part, g), 0, unroll=2)
-            lax.fori_loop(0, chunks, functools.partial(state_part, g), 0, unroll=4)
+            lax.fori_loop(0, chunks, functools.partial(conv_part, g), 0, unroll=4)
+            lax.fori_loop(0, chunks, functools.partial(state_part, g), 0, unroll=8)
             send_states(g)
             for ready in SCAN_AFTER_SENDING[g]:
                 scan_states(ready)
 
     def inner_part(c, _):
         info = cols[rows_of(c)]
-        gate_copy(c).wait()
 
         masked = scores[c]
         r = r_enter[rows_of(c)]
@@ -386,7 +385,9 @@
         return 0
 
     if phases >= 4:
-        lax.fori_loop(0, chunks, read_part, 0, unroll=2)
+        lax.fori_loop(0, chunks, read_part, 0, unroll=4)
+        for c in range(chunks):
+            gate_copy(c).wait()
         done = 0
         for until, ready in [*SCAN_AFTER_INNER.items(), (chunks, ())]:
             lax.fori_loop(done, until, inner_part, 0)
@@ -422,7 +423,7 @@
         assemble(g)
 
     if phases >= 5:
-        lax.fori_loop(0, chunks, finish_part, 0)
+        lax.fori_loop(0, chunks, finish_part, 0, unroll=2)
 
     total = sq[...]
     if comm:

time: 71.2 us -> 69 us (0.969)
  Pallas kernels: 70.8 us -> 68.6 us
    pallas_call x1, Pallas kernels: 63.4 us -> 61.2 us  [main_call(): pl.pallas_call(functools.partial(main_kernel, n_seq, n_head, comm, phases...]
where the time goes in v7:
time: 69 us; the launch traced here: 68.8 us
  Pallas kernels  68.6 us (99%)
    pallas_call x1, Pallas kernels, main_call(): pl.pallas_call(functools.partial(main_kernel, n_seq, n_head, comm, phases...  61.2 us
    pallas_call x1, Pallas kernels, norm_call(): pl.pallas_call(norm_kernel, in_specs=[hbm, vmem, vmem], out_specs=hbm, ou...  7.44 us

profile of v7, /device:TPU:1, one launch (start us, length us, event | category | flops | bytes accessed | tf_op | source)
XLA Modules:
  0.0 68.8 jit_solution(6124740359916672796)
XLA Ops:
  0.0 61.2 %main.1 = (bf16[2048,2048]{1,0:T(8,128)(2,1)}, f32[8,2,128]{2,1,0:T(2,128)}) custom-call(bf16[2048,2048]{1,0:T(8,128)(2,1)} %x_hbm.1, bf16[2048,2048]{1,0:T(8,128)(2,1)} %gate_hbm.1, bf16[2048,128]{1,0:T(8,128)(2,1)} %write_ref.1, bf16[2048,128]{1,0:T(8,128)(2,1)} %read_ref.1, f32[16,2048]{1,0:T(8,128)} %step_ref.1, f32[1,16]{1,0:T(1,128)} %bitcast.7, ...), custom_call_target="tpu_custom_call" | custom-call | tf_op jit(solution)/shard_map/main/pallas_call | solution.py:466
  61.2 7.4 %norm.1 = bf16[2048,2048]{1,0:T(8,128)(2,1)} custom-call(bf16[2048,2048]{1,0:T(8,128)(2,1)} %get-tuple-element.7.gated_hbm, f32[8,2,128]{2,1,0:T(2,128)} %get-tuple-element.8.scale_ref, f32[1,2048]{1,0:T(1,128)} %bitcast.6), custom_call_target="tpu_custom_call" | custom-call | tf_op jit(solution)/shard_map/norm/pallas_call | solution.py:551
